TPU v7x, 32 devices: a whole 2x2x4 slice. The times are simulated.
32 devices in a mesh: ctx: 4 (over z), fsdp: 8 (over y, x, core).
Axes of the slice: x: 2, y: 2, z: 4, core: 2. Of those that a mesh axis runs over, the one named last changes fastest.
Arguments:
- hidden_in: bfloat16 [24, 1024, 768], P('fsdp', 'ctx'), may hold values from -6 to 6
- attn_gain: bfloat16 [768], P('fsdp'), may hold values from 0.099609375 to 1.8984375
- attn_shift: bfloat16 [768], P('fsdp'), may hold values from -1.75 to 1.75
- query_key_value_weight: bfloat16 [768, 2304], P('fsdp'), may hold values from -0.21875 to 0.21875
- query_bias: bfloat16 [768], P('fsdp'), may hold values from -1.75 to 1.75
- value_bias: bfloat16 [768], P('fsdp'), may hold values from -1.75 to 1.75
- projection_output_weight: bfloat16 [768, 768], P('fsdp'), may hold values from -1.75 to 1.75
- projection_output_bias: bfloat16 [768], P('fsdp'), may hold values from -1.75 to 1.75
- mlp_gain: bfloat16 [768], P('fsdp'), may hold values from 0.099609375 to 1.8984375
- mlp_shift: bfloat16 [768], P('fsdp'), may hold values from -1.75 to 1.75
- up_projection_weight: bfloat16 [768, 3072], P('fsdp'), may hold values from -0.21875 to 0.21875
- up_projection_bias: bfloat16 [3072], P('fsdp'), may hold values from -1.75 to 1.75
- down_projection_weight: bfloat16 [3072, 768], P('fsdp'), may hold values from -0.109375 to 0.109375
- down_projection_bias: bfloat16 [768], P('fsdp'), may hold values from -1.75 to 1.75
- out_grad: bfloat16 [24, 1024, 768], P('fsdp', 'ctx'), may hold values from -8 to 8
Outputs:
- block_out: bfloat16 [24, 1024, 768], P('fsdp', 'ctx')
- input_grad: bfloat16 [24, 1024, 768], P('fsdp', 'ctx')
- attn_gain_grad: float32 [768], P('fsdp')
- attn_shift_grad: float32 [768], P('fsdp')
- qkv_grad: float32 [768, 2304], P('fsdp')
- query_bias_grad: float32 [768], P('fsdp')
- value_bias_grad: float32 [768], P('fsdp')
- proj_grad: float32 [768, 768], P('fsdp')
- proj_bias_grad: float32 [768], P('fsdp')
- mlp_gain_grad: float32 [768], P('fsdp')
- mlp_shift_grad: float32 [768], P('fsdp')
- up_grad: float32 [768, 3072], P('fsdp')
- up_bias_grad: float32 [3072], P('fsdp')
- down_grad: float32 [3072, 768], P('fsdp')
- down_bias_grad: float32 [768], P('fsdp')
- softmax_stats: float32 [24, 12, 1024], P('fsdp', None, 'ctx')
All inputs are finite; a program needn't handle non-finite values.
Results may differ from a plain program's by a relative error of at most 0.033.
Values may be sent and summed in bfloat16 or wider, within the bound.
A program may use at most 192 MiB of HBM per device.

v0:
```python
from functools import partial

import jax
import jax.numpy as jnp
from jax import lax
from jax.sharding import PartitionSpec as P

HEADS = 12
HD = 64


NEG_BIG = -1e30


def as_sent(value):
    return jax.tree.map(lambda a: a.astype(jnp.bfloat16) if a.dtype == jnp.float32 else a, value)


def layer_norm(values, gain, shift):
    center = values - jnp.mean(values, axis=-1, keepdims=True)
    spread = jnp.mean(center * center, axis=-1, keepdims=True)
    return center * lax.rsqrt(spread + 1e-05) * gain + shift


def exact_gelu(values):
    return jax.nn.gelu(values, approximate=False)


def split_heads(values):
    return values.reshape(values.shape[0], values.shape[1], HEADS, HD)


def forward_block(carry_state, blocks, key_start, queries, query_pos):
    keys_blk, values_blk = blocks

    def forward_update(unused):
        run_max, run_sum, accumulated = carry_state
        scores = jnp.einsum(
            "sbhe,snhe->shbn", queries, split_heads(keys_blk), preferred_element_type=jnp.float32
        )
        key_pos = key_start + jnp.arange(keys_blk.shape[1])
        visible = query_pos[:, None] >= key_pos[None, :]
        scores = jnp.where(visible, scores, NEG_BIG)
        new_max = jnp.maximum(run_max, jnp.max(scores, axis=-1))
        weights = jnp.where(visible, jnp.exp(scores - new_max[..., None]), 0.0)
        factor = jnp.exp(run_max - new_max)
        new_sum = run_sum * factor + jnp.sum(weights, axis=-1)
        new_acc = accumulated * factor[..., None] + jnp.einsum(
            "shbn,snhe->shbe",
            weights.astype(jnp.bfloat16),
            split_heads(values_blk),
            preferred_element_type=jnp.float32,
        )
        return (new_max, new_sum, new_acc)

    return lax.cond(key_start > query_pos[-1], lambda unused: carry_state, forward_update, None)


def query_block(carry_state, blocks, key_start, queries, grad_out, row_stats, row_delta, query_pos):
    keys_blk, values_blk = blocks

    def query_update(unused):
        query_grad = carry_state[0]
        key_heads = split_heads(keys_blk)
        scores = jnp.einsum(
            "sbhe,snhe->shbn", queries, key_heads, preferred_element_type=jnp.float32
        )
        key_pos = key_start + jnp.arange(keys_blk.shape[1])
        visible = query_pos[:, None] >= key_pos[None, :]
        probability = jnp.where(visible, jnp.exp(scores - row_stats[..., None]), 0.0)
        prob_grad = jnp.einsum(
            "sbhe,snhe->shbn", grad_out, split_heads(values_blk), preferred_element_type=jnp.float32
        )
        score_grad = (probability * (prob_grad - row_delta[..., None])).astype(jnp.bfloat16)
        return (
            query_grad
            + jnp.einsum(
                "shbn,snhe->shbe", score_grad, key_heads, preferred_element_type=jnp.float32
            ),
        )

    return lax.cond(key_start > query_pos[-1], lambda unused: carry_state, query_update, None)


def key_block(
    carry_state,
    query_blk,
    grad_blk,
    stats_blk,
    delta_blk,
    query_start,
    key_heads,
    value_heads,
    key_pos,
):
    query_pos = query_start + jnp.arange(query_blk.shape[1])

    def key_update(unused):
        key_grad, value_grad = carry_state
        stats_now = jnp.transpose(stats_blk, (0, 2, 1))
        delta_now = jnp.transpose(delta_blk, (0, 2, 1))
        scores = jnp.einsum(
            "sbhe,snhe->shbn", query_blk, key_heads, preferred_element_type=jnp.float32
        )
        visible = query_pos[:, None] >= key_pos[None, :]
        probability = jnp.where(visible, jnp.exp(scores - stats_now[..., None]), 0.0)
        value_grad = value_grad + jnp.einsum(
            "shbn,sbhe->snhe",
            probability.astype(jnp.bfloat16),
            grad_blk,
            preferred_element_type=jnp.float32,
        )
        prob_grad = jnp.einsum(
            "sbhe,snhe->shbn", grad_blk, value_heads, preferred_element_type=jnp.float32
        )
        score_grad = (probability * (prob_grad - delta_now[..., None])).astype(jnp.bfloat16)
        key_grad = key_grad + jnp.einsum(
            "shbn,sbhe->snhe", score_grad, query_blk, preferred_element_type=jnp.float32
        )
        return (key_grad, value_grad)

    return lax.cond(query_pos[-1] < key_pos[0], lambda unused: carry_state, key_update, None)


def sweep_blocks(carry_state, arrays, first_row, block_rows, step):
    block_count = arrays[0].shape[1] // block_rows

    def one_block(block_num, carry):
        offset = block_num * block_rows
        blocks = tuple((lax.dynamic_slice_in_dim(array, offset, block_rows, 1) for array in arrays))
        return step(carry, blocks, first_row + offset)

    return lax.fori_loop(0, block_count, one_block, carry_state)


def local(
    hidden_in,
    attn_gain,
    attn_shift,
    query_key_value_weight,
    query_bias,
    value_bias,
    projection_output_weight,
    projection_output_bias,
    mlp_gain,
    mlp_shift,
    up_projection_weight,
    up_projection_bias,
    down_projection_weight,
    down_projection_bias,
    out_grad,
):
    (
        attn_gain_all,
        attn_shift_all,
        qkv_weight_all,
        query_bias_all,
        value_bias_all,
        proj_weight_all,
        proj_bias_all,
        mlp_gain_all,
        mlp_shift_all,
        up_weight_all,
        up_bias_all,
        down_weight_all,
        down_bias_all,
    ) = (
        lax.all_gather(attn_gain, "fsdp", axis=0, tiled=True),
        lax.all_gather(attn_shift, "fsdp", axis=0, tiled=True),
        lax.all_gather(query_key_value_weight, "fsdp", axis=0, tiled=True),
        lax.all_gather(query_bias, "fsdp", axis=0, tiled=True),
        lax.all_gather(value_bias, "fsdp", axis=0, tiled=True),
        lax.all_gather(projection_output_weight, "fsdp", axis=0, tiled=True),
        lax.all_gather(projection_output_bias, "fsdp", axis=0, tiled=True),
        lax.all_gather(mlp_gain, "fsdp", axis=0, tiled=True),
        lax.all_gather(mlp_shift, "fsdp", axis=0, tiled=True),
        lax.all_gather(up_projection_weight, "fsdp", axis=0, tiled=True),
        lax.all_gather(up_projection_bias, "fsdp", axis=0, tiled=True),
        lax.all_gather(down_projection_weight, "fsdp", axis=0, tiled=True),
        lax.all_gather(down_projection_bias, "fsdp", axis=0, tiled=True),
    )
    seqs_here, block_rows, feature_count = hidden_in.shape
    row_count = seqs_here * block_rows
    hidden = hidden_in.astype(jnp.float32).reshape(row_count, feature_count)
    normed_input, attn_back = jax.vjp(
        layer_norm, hidden, attn_gain_all.astype(jnp.float32), attn_shift_all.astype(jnp.float32)
    )
    normed_low = normed_input.astype(jnp.bfloat16)
    joined_heads = jnp.dot(normed_low, qkv_weight_all, preferred_element_type=jnp.float32)
    queries = (
        (joined_heads[:, :feature_count] + query_bias_all.astype(jnp.float32)) * 0.125
    ).astype(jnp.bfloat16)
    key_rows = joined_heads[:, feature_count : 2 * feature_count].astype(jnp.bfloat16)
    values = (joined_heads[:, 2 * feature_count :] + value_bias_all.astype(jnp.float32)).astype(
        jnp.bfloat16
    )
    query_heads = queries.reshape(seqs_here, block_rows, HEADS, HD)
    keys_seq = key_rows.reshape(seqs_here, block_rows, feature_count)
    values_seq = values.reshape(seqs_here, block_rows, feature_count)
    query_pos = lax.axis_index("ctx") * block_rows + jnp.arange(block_rows)
    start_state = (
        jnp.full((seqs_here, HEADS, block_rows), NEG_BIG, jnp.float32),
        jnp.zeros((seqs_here, HEADS, block_rows), jnp.float32),
        jnp.zeros((seqs_here, HEADS, block_rows, HD), jnp.float32),
    )
    forward_step = partial(forward_block, queries=query_heads, query_pos=query_pos)
    keys_all, values_all = (
        lax.all_gather(keys_seq, "ctx", axis=1, tiled=True),
        lax.all_gather(values_seq, "ctx", axis=1, tiled=True),
    )
    run_max, run_sum, accumulated = sweep_blocks(
        start_state, (keys_all, values_all), 0, block_rows, forward_step
    )
    row_stats = run_max + jnp.log(run_sum)
    attended_rows = accumulated / run_sum[..., None]
    attended_low = (
        jnp.transpose(attended_rows, (0, 2, 1, 3))
        .reshape(row_count, feature_count)
        .astype(jnp.bfloat16)
    )
    middle_residual = (
        hidden
        + jnp.dot(attended_low, proj_weight_all, preferred_element_type=jnp.float32)
        + proj_bias_all.astype(jnp.float32)
    )
    second_normed, mlp_back = jax.vjp(
        layer_norm,
        middle_residual,
        mlp_gain_all.astype(jnp.float32),
        mlp_shift_all.astype(jnp.float32),
    )
    second_low = second_normed.astype(jnp.bfloat16)
    inner_preactivation = jnp.dot(
        second_low, up_weight_all, preferred_element_type=jnp.float32
    ) + up_bias_all.astype(jnp.float32)
    active_hidden, gelu_back = jax.vjp(exact_gelu, inner_preactivation)
    active_low = active_hidden.astype(jnp.bfloat16)
    block_result = (
        middle_residual
        + jnp.dot(active_low, down_weight_all, preferred_element_type=jnp.float32)
        + down_bias_all.astype(jnp.float32)
    )
    block_out = block_result.astype(jnp.bfloat16).reshape(seqs_here, block_rows, feature_count)
    qkv_back, proj_back, up_back, down_back = (
        lax.all_gather(query_key_value_weight, "fsdp", axis=0, tiled=True),
        lax.all_gather(projection_output_weight, "fsdp", axis=0, tiled=True),
        lax.all_gather(up_projection_weight, "fsdp", axis=0, tiled=True),
        lax.all_gather(down_projection_weight, "fsdp", axis=0, tiled=True),
    )
    grad_top = out_grad.astype(jnp.float32).reshape(row_count, feature_count)
    branch_down = grad_top.astype(jnp.bfloat16)
    down_grad = jnp.einsum("rf,rd->fd", active_low, branch_down, preferred_element_type=jnp.float32)
    down_bias_grad = jnp.sum(branch_down, axis=0, dtype=jnp.float32)
    grad_active = jnp.einsum(
        "rd,fd->rf", branch_down, down_back, preferred_element_type=jnp.float32
    )
    inner_grad = gelu_back(grad_active)[0].astype(jnp.bfloat16)
    up_grad = jnp.einsum("rd,rf->df", second_low, inner_grad, preferred_element_type=jnp.float32)
    up_bias_grad = jnp.sum(inner_grad, axis=0, dtype=jnp.float32)
    grad_second = jnp.einsum("rf,df->rd", inner_grad, up_back, preferred_element_type=jnp.float32)
    grad_middle, mlp_gain_grad, mlp_shift_grad = mlp_back(grad_second)
    grad_middle = grad_middle + grad_top
    branch_up = grad_middle.astype(jnp.bfloat16)
    proj_grad = jnp.einsum("rd,re->de", attended_low, branch_up, preferred_element_type=jnp.float32)
    proj_bias_grad = jnp.sum(branch_up, axis=0, dtype=jnp.float32)
    att_grad = jnp.einsum(
        "re,de->rd", branch_up, proj_back, preferred_element_type=jnp.float32
    ).astype(jnp.bfloat16)
    grad_heads = att_grad.reshape(seqs_here, block_rows, HEADS, HD)
    row_delta = jnp.sum(
        attended_rows * jnp.transpose(grad_heads, (0, 2, 1, 3)).astype(jnp.float32), axis=-1
    )
    query_zero = jnp.zeros((seqs_here, HEADS, block_rows, HD), jnp.float32)
    back_state = (query_zero,)
    backward_step = partial(
        query_block,
        queries=query_heads,
        grad_out=grad_heads,
        row_stats=row_stats,
        row_delta=row_delta,
        query_pos=query_pos,
    )
    back_result = sweep_blocks(back_state, (keys_all, values_all), 0, block_rows, backward_step)
    query_grad = back_result[0]
    stats_all, delta_all = (
        lax.all_gather(
            jnp.transpose(row_stats, (0, 2, 1)).astype(jnp.bfloat16), "ctx", axis=1, tiled=True
        ).astype(jnp.float32),
        lax.all_gather(
            jnp.transpose(row_delta, (0, 2, 1)).astype(jnp.bfloat16), "ctx", axis=1, tiled=True
        ).astype(jnp.float32),
    )
    own_keys = split_heads(keys_seq)
    own_values = split_heads(values_seq)

    def key_step(carry_state, blocks, query_start):
        stats_blk = lax.dynamic_slice_in_dim(stats_all, query_start, block_rows, 1)
        delta_blk = lax.dynamic_slice_in_dim(delta_all, query_start, block_rows, 1)
        return key_block(
            carry_state,
            blocks[0],
            blocks[1],
            stats_blk,
            delta_blk,
            query_start,
            own_keys,
            own_values,
            query_pos,
        )

    key_zero = jnp.zeros((seqs_here, block_rows, HEADS, HD), jnp.float32)
    key_grad_own, value_grad_own = sweep_blocks(
        (key_zero, key_zero),
        (
            lax.all_gather(query_heads, "ctx", axis=1, tiled=True),
            lax.all_gather(grad_heads, "ctx", axis=1, tiled=True),
        ),
        jnp.int32(0),
        block_rows,
        key_step,
    )
    key_grad_sum = key_grad_own.reshape(seqs_here, block_rows, feature_count)
    value_grad_sum = value_grad_own.reshape(seqs_here, block_rows, feature_count)
    query_grad_low = (
        jnp.transpose(query_grad, (0, 2, 1, 3))
        .reshape(row_count, feature_count)
        .astype(jnp.bfloat16)
    )
    key_grad_low = key_grad_sum.reshape(row_count, feature_count).astype(jnp.bfloat16)
    value_grad_low = value_grad_sum.reshape(row_count, feature_count).astype(jnp.bfloat16)
    joined_grad = jnp.concatenate(
        [
            (query_grad_low.astype(jnp.float32) * 0.125).astype(jnp.bfloat16),
            key_grad_low,
            value_grad_low,
        ],
        axis=1,
    )
    qkv_grad = jnp.einsum("rd,rf->df", normed_low, joined_grad, preferred_element_type=jnp.float32)
    query_bias_grad = jnp.sum(query_grad_low, axis=0, dtype=jnp.float32) * 0.125
    value_bias_grad = jnp.sum(value_grad_low, axis=0, dtype=jnp.float32)
    grad_normed = jnp.einsum("rf,df->rd", joined_grad, qkv_back, preferred_element_type=jnp.float32)
    grad_hidden, attn_gain_grad, attn_shift_grad = attn_back(grad_normed)
    input_grad = (
        (grad_middle + grad_hidden)
        .astype(jnp.bfloat16)
        .reshape(seqs_here, block_rows, feature_count)
    )
    summed = (
        lax.psum_scatter(
            attn_gain_grad.astype(jnp.bfloat16), "fsdp", scatter_dimension=0, tiled=True
        ).astype(jnp.float32),
        lax.psum_scatter(
            attn_shift_grad.astype(jnp.bfloat16), "fsdp", scatter_dimension=0, tiled=True
        ).astype(jnp.float32),
        lax.psum_scatter(
            qkv_grad.astype(jnp.bfloat16), "fsdp", scatter_dimension=0, tiled=True
        ).astype(jnp.float32),
        lax.psum_scatter(
            query_bias_grad.astype(jnp.bfloat16), "fsdp", scatter_dimension=0, tiled=True
        ).astype(jnp.float32),
        lax.psum_scatter(
            value_bias_grad.astype(jnp.bfloat16), "fsdp", scatter_dimension=0, tiled=True
        ).astype(jnp.float32),
        lax.psum_scatter(
            proj_grad.astype(jnp.bfloat16), "fsdp", scatter_dimension=0, tiled=True
        ).astype(jnp.float32),
        lax.psum_scatter(
            proj_bias_grad.astype(jnp.bfloat16), "fsdp", scatter_dimension=0, tiled=True
        ).astype(jnp.float32),
        lax.psum_scatter(
            mlp_gain_grad.astype(jnp.bfloat16), "fsdp", scatter_dimension=0, tiled=True
        ).astype(jnp.float32),
        lax.psum_scatter(
            mlp_shift_grad.astype(jnp.bfloat16), "fsdp", scatter_dimension=0, tiled=True
        ).astype(jnp.float32),
        lax.psum_scatter(
            up_grad.astype(jnp.bfloat16), "fsdp", scatter_dimension=0, tiled=True
        ).astype(jnp.float32),
        lax.psum_scatter(
            up_bias_grad.astype(jnp.bfloat16), "fsdp", scatter_dimension=0, tiled=True
        ).astype(jnp.float32),
        lax.psum_scatter(
            down_grad.astype(jnp.bfloat16), "fsdp", scatter_dimension=0, tiled=True
        ).astype(jnp.float32),
        lax.psum_scatter(
            down_bias_grad.astype(jnp.bfloat16), "fsdp", scatter_dimension=0, tiled=True
        ).astype(jnp.float32),
    )
    summed = jax.tree.map(
        lambda part: part.astype(jnp.float32), lax.psum(as_sent(tuple(summed)), "ctx")
    )
    return (block_out, input_grad) + tuple(summed) + (row_stats,)


def solution(mesh):
    placed = (
        P("fsdp", "ctx", None),
        P("fsdp"),
        P("fsdp"),
        P("fsdp", None),
        P("fsdp"),
        P("fsdp"),
        P("fsdp", None),
        P("fsdp"),
        P("fsdp"),
        P("fsdp"),
        P("fsdp", None),
        P("fsdp"),
        P("fsdp", None),
        P("fsdp"),
        P("fsdp", "ctx", None),
    )
    return jax.shard_map(
        local,
        mesh=mesh,
        in_specs=placed,
        out_specs=(
            P("fsdp", "ctx", None),
            P("fsdp", "ctx", None),
            P("fsdp"),
            P("fsdp"),
            P("fsdp", None),
            P("fsdp"),
            P("fsdp"),
            P("fsdp", None),
            P("fsdp"),
            P("fsdp"),
            P("fsdp"),
            P("fsdp", None),
            P("fsdp"),
            P("fsdp", None),
            P("fsdp"),
            P("fsdp", None, "ctx"),
        ),
        check_vma=False,
    )
```

profile of v0, /device:TPU:0, one launch (start us, length us, event | category | flops | bytes accessed | tf_op | source)
XLA Modules:
  0.0 873.0 jit_solution(1653293870865556197)
XLA Ops:
  15.8 26.0 %all-reduce.18 = (bf16[768]{0:T(1024)(128)(2,1)S(1)}, bf16[768]{0:T(1024)(128)(2,1)S(1)}, bf16[768]{0:T(1024)(128)(2,1)S(1)}, bf16[768]{0:T(1024)(128)(2,1)S(1)}...) all-reduce(bf16[768]{0:T(1024)(128)(2,1)S(1)} %dynamic-update-slice, ...), channel_id=1, replica_groups=mesh['ctx'=4,'fsdp'=8] {'fsdp'}, use_global_device_ids=true, to_apply=%add.1 | all-reduce | flops 5376 | bytes 21504
  46.8 4.9 fusion.86
  65.1 8.7 %all-gather = bf16[8,1,384]{2,1,0:T(2,128)(2,1)S(1)} all-gather(bf16[1,1,384]{2,1,0:T(2,128)(2,1)S(1)} %reshape.242), channel_id=1, replica_groups=mesh['ctx'=4,'fsdp'=8] {'fsdp'}, dimensions={0}, use_global_device_ids=true | all-gather | bytes 6912 | tf_op jit(solution)/shard_map/all_gather | solution.py:178
  78.4 67.0 %all-gather.12.cloned.1.call-done = bf16[3,1024,768]{1,2,0:T(8,128)(2,1)} async-done(((bf16[3,256,768]{1,2,0:T(8,128)(2,1)}), bf16[3,1024,768]{1,2,0:T(8,128)(2,1)}) %all-gather.12.cloned.1.call-update) | async-done | bytes 4718608 | tf_op jit(solution)/shard_map/all_gather | solution.py:208
  145.4 89.5 %all-gather.14.cloned.1.call-done = bf16[3,1024,768]{1,2,0:T(8,128)(2,1)} async-done(((bf16[3,256,768]{1,2,0:T(8,128)(2,1)}), bf16[3,1024,768]{1,2,0:T(8,128)(2,1)}) %all-gather.14.cloned.1.call-update) | async-done | bytes 4718608 | tf_op jit(solution)/shard_map/all_gather | solution.py:209
  236.6 14.9 %while.48 = (s32[]{:T(128)}, f32[3,12,256]{2,1,0:T(8,128)S(1)}, f32[3,12,256]{2,1,0:T(8,128)S(1)}, f32[3,12,256,64]{2,3,1,0:T(8,128)}, s32[256]{0:T(256)S(1)}, /...) while((s32[]{:T(128)}, f32[3,12,256]{2,1,0:T(8,128)S(1)}, ...), condition=%wide.region_7.8_spmd, body=%wide.region_2.7_spmd.sunk | while | flops 628836608 | bytes 61017440 | solution.py:133
  237.8 9.3 %conditional.6 = (f32[3,12,256]{2,1,0:T(8,128)S(1)}, f32[3,12,256]{2,1,0:T(8,128)S(1)}, f32[3,12,256,64]{2,3,1,0:T(8,128)}) conditional(s32[]{:T(128)} %convert_element_type.429, (s32[256]{0:T(256)S(1)}, s32[]{:T(128)}, bf16[3,1024,768]{1,2,0:T(8,128)(2,1)}, bf16[3,256,12,64]{1,3,2,0:T(8,128)(2,1)S(1)}, f32[3,12,256]{2,1,0:T(8,128)S(1)}, ...), branch_computations={%region_3.5_spmd, %region_6.6_spmd} | conditional | flops 628836608 | bytes 60943484 | solution.py:56
  263.9 35.7 %all-gather.18.cloned.1.call-done = bf16[768,3072]{1,0:T(8,128)(2,1)} async-done(((bf16[96,3072]{1,0:T(8,128)(2,1)}), bf16[768,3072]{1,0:T(8,128)(2,1)}) %all-gather.18.cloned.1.call-update) | async-done | bytes 4718608 | tf_op jit(solution)/shard_map/all_gather | solution.py:177
  299.6 10.7 %fusion.75 = f32[768,3072]{1,0:T(8,128)} fusion(bf16[768,3072]{1,0:T(8,128)(2,1)} %all-gather.18.cloned.1.call-done, f32[768,768]{1,0:T(8,128)} %copy-done.17, f32[768]{0:T(1024)S(1)} %copy-done.58, f32[768]{0:T(1024)S(1)} %copy-done.53, f32[768]{0:T(1024)S(1)} %fusion.72, f32[768]{0:T(1024)S(1)} %broadcast_multiply_fusion), kind=kOutput, calls=%fused_computation.137 | convolution fusion | flops 3626827776 | bytes 16527360 | tf_op jit(solution)/shard_map/dot_general | solution.py:233
  310.4 30.0 %all-gather.20.cloned.1.call-done = bf16[3072,768]{1,0:T(8,128)(2,1)} async-done(((bf16[384,768]{1,0:T(8,128)(2,1)}), bf16[3072,768]{1,0:T(8,128)(2,1)}) %all-gather.20.cloned.1.call-update) | async-done | bytes 4718608 | tf_op jit(solution)/shard_map/all_gather | solution.py:179
  340.3 29.5 %fusion.77 = (bf16[3072]{0:T(1024)(128)(2,1)}, bf16[768,3072]{1,0:T(8,128)(2,1)S(1)}, f32[768,3072]{1,0:T(8,128)}) fusion(f32[768,3072]{1,0:T(8,128)} %fusion.75, f32[3072]{0:T(1024)S(1)} %bitcast.174, bf16[768,768]{1,0:T(8,128)(2,1)S(1)} %bitcast.160, bf16[3072,768]{1,0:T(8,128)(2,1)} %all-gather.20.cloned.1.call-done), kind=kOutput, calls=%fused_computation.139 | convolution fusion | flops 3798463488 | bytes 29509632 | tf_op jit(solution)/shard_map/rd,fd->rf/dot_general | solution.py:254
  369.9 4.8 multiply_reduce_fusion
  390.2 8.3 convolution_convert_fusion.2
  398.5 10.9 %multiply_convert_fusion.4 = bf16[768,3072]{1,0:T(8,128)(2,1)} fusion(f32[768,3072]{1,0:T(8,128)} %get-tuple-element.1021, f32[768,3072]{1,0:T(8,128)} %fusion.75, f32[3072]{0:T(1024)S(1)} %bitcast.175), kind=kLoop, calls=%fused_computation.60 | loop fusion | flops 9437184 | bytes 23605248 | tf_op jit(solution)/shard_map/convert_element_type | solution.py:237
  409.4 8.1 convolution_convert_fusion.1
  421.4 4.7 reshape.262
  428.9 4.7 copy.77
  440.8 22.2 %while.49 = (s32[]{:T(128)}, f32[3,12,256,64]{2,3,1,0:T(8,128)}, s32[256]{0:T(256)S(1)}, bf16[3,1024,768]{1,2,0:T(8,128)(2,1)}, bf16[3,256,12,64]{1,3,2,0:T(8,12...) while((s32[]{:T(128)}, f32[3,12,256,64]{2,3,1,0:T(8,128)}, ...), condition=%wide.region_16.17_spmd, body=%wide.region_13.16_spmd.sunk | while | flops 918421760 | bytes 34417936 | solution.py:133
  442.0 17.1 %conditional.7 = (f32[3,12,256,64]{2,3,1,0:T(8,128)}) conditional(s32[]{:T(128)} %convert_element_type.430, (s32[256]{0:T(256)S(1)}, s32[]{:T(128)}, bf16[3,1024,768]{1,2,0:T(8,128)(2,1)}, bf16[3,256,12,64]{1,3,2,0:T(8,128)(2,1)S(1)}, f32[3,12,256]{2,1,0:T(8,128)}, /*index=5*/bf16[3,1024,768]{1,2,0:T(8,128)(2,1)}, ...), branch_computations={%region_14.14_spmd, %region_15.15_spmd} | conditional | flops 918421760 | bytes 34417712 | solution.py:82
  443.9 5.1 fusion.85
  449.7 9.5 %fusion.19 = f32[3,12,256,64]{2,3,1,0:T(8,128)} fusion(f32[3,12,256,64]{2,3,1,0:T(8,128)} %get-tuple-element.783, bf16[3,256,12,64]{1,3,2,0:T(8,128)(2,1)S(1)} %bitcast.156, f32[3,12,256,256]{3,2,1,0:T(8,128)} %fusion.85, f32[3,12,256]{2,1,0:T(8,128)} %get-tuple-element.791, f32[3,12,256]{2,1,0:T(8,128)} %get-tuple-element.788, ...), kind=kOutput, calls=%fused_computation.25 | convolution fusion | flops 616366080 | bytes 17833984 | tf_op jit(solution)/shard_map/while/body/eval_jaxpr/cond/branch_0_fun/shbn,snhe->shbe/dot_general | solution.py:77
  466.5 75.0 %all_gather.77 = bf16[3,1024,12]{1,2,0:T(8,128)(2,1)S(1)} all-gather(bf16[3,256,12]{1,2,0:T(8,128)(2,1)S(1)} %copy-done.37), channel_id=1, replica_groups=mesh['ctx'=4,'fsdp'=8] {'ctx'}, dimensions={1}, use_global_device_ids=true | all-gather | bytes 92160 | tf_op jit(solution)/shard_map/all_gather | solution.py:286
  542.2 20.2 %all_gather.79 = bf16[3,1024,12]{1,0,2:T(4,128)(2,1)S(1)} all-gather(bf16[3,256,12]{1,0,2:T(4,128)(2,1)S(1)} %convert_bitcast_fusion), channel_id=1, replica_groups=mesh['ctx'=4,'fsdp'=8] {'ctx'}, dimensions={1}, use_global_device_ids=true | all-gather | bytes 92160 | tf_op jit(solution)/shard_map/all_gather | solution.py:289
  563.1 6.8 copy.74
  574.5 6.8 copy.76
  583.3 101.5 %while.50 = (s32[]{:T(128)}, f32[3,256,12,64]{1,3,2,0:T(8,128)}, f32[3,256,12,64]{1,3,2,0:T(8,128)S(1)}, s32[256]{0:T(256)S(1)}, bf16[3,1024,12,64]{1,3,2,0:T(8,...) while((s32[]{:T(128)}, f32[3,256,12,64]{1,3,2,0:T(8,128)}, ...), condition=%wide.region_20.21_spmd, body=%wide.region_17.20_spmd.sunk | while | flops 1228079360 | bytes 45322584 | solution.py:133
  585.7 22.5 %conditional.8 = ((f32[3,256,12,64]{1,3,2,0:T(8,128)}, f32[3,256,12,64]{1,3,2,0:T(8,128)S(1)})) conditional(s32[]{:T(128)} %bitcast.154, (s32[256]{0:T(256)S(1)}, s32[256]{0:T(256)S(1)}, s32[]{:T(128)}, bf16[3,1024,12,64]{1,3,2,0:T(8,128)(2,1)}, bf16[3,256,12,64]{1,3,2,0:T(8,128)(2,1)S(1)}, /*index=5*/f32[3,1024,12]{1,2,0:T(8,128)}, ...), branch_computations={%region_18.18_spmd, %region_19.19_spmd} | conditional | flops 1228079104 | bytes 45321288 | solution.py:122
  585.7 6.4 fusion.39
  594.3 8.7 bitcast_add_fusion.1
  603.0 5.2 bitcast_add_fusion
  610.6 23.6 %conditional.8 = ((f32[3,256,12,64]{1,3,2,0:T(8,128)}, f32[3,256,12,64]{1,3,2,0:T(8,128)S(1)})) conditional(s32[]{:T(128)} %bitcast.154, (s32[256]{0:T(256)S(1)}, s32[256]{0:T(256)S(1)}, s32[]{:T(128)}, bf16[3,1024,12,64]{1,3,2,0:T(8,128)(2,1)}, bf16[3,256,12,64]{1,3,2,0:T(8,128)(2,1)S(1)}, /*index=5*/f32[3,1024,12]{1,2,0:T(8,128)}, ...), branch_computations={%region_18.18_spmd, %region_19.19_spmd} | conditional | flops 1228079104 | bytes 45321288 | solution.py:122
  610.6 6.4 fusion.39
  619.2 9.4 %bitcast_add_fusion.1 = f32[3,256,12,64]{1,3,2,0:T(8,128)} fusion(f32[3,256,12,64]{1,3,2,0:T(8,128)} %get-tuple-element.802, f32[3,12,256,256]{3,2,1,0:T(8,128)} %fusion.39, f32[3,12,256]{2,1,0:T(8,128)} %get-tuple-element.1032, f32[3,12,256]{2,1,0:T(8,128)} %get-tuple-element.1033, pred[256,256]{1,0:T(8,128)(4,1)} %broadcast_compare_fusion.2, ...), kind=kOutput, calls=%fused_computation.42 | convolution fusion | flops 616366080 | bytes 17859584 | tf_op jit(solution)/shard_map/while/body/eval_jaxpr/cond/branch_0_fun/shbn,sbhe->snhe/dot_general | solution.py:117
  628.6 5.6 bitcast_add_fusion
  636.6 22.5 %conditional.8 = ((f32[3,256,12,64]{1,3,2,0:T(8,128)}, f32[3,256,12,64]{1,3,2,0:T(8,128)S(1)})) conditional(s32[]{:T(128)} %bitcast.154, (s32[256]{0:T(256)S(1)}, s32[256]{0:T(256)S(1)}, s32[]{:T(128)}, bf16[3,1024,12,64]{1,3,2,0:T(8,128)(2,1)}, bf16[3,256,12,64]{1,3,2,0:T(8,128)(2,1)S(1)}, /*index=5*/f32[3,1024,12]{1,2,0:T(8,128)}, ...), branch_computations={%region_18.18_spmd, %region_19.19_spmd} | conditional | flops 1228079104 | bytes 45321288 | solution.py:122
  636.6 6.3 fusion.39
  645.1 8.7 bitcast_add_fusion.1
  653.8 5.3 bitcast_add_fusion
  661.6 23.2 %conditional.8 = ((f32[3,256,12,64]{1,3,2,0:T(8,128)}, f32[3,256,12,64]{1,3,2,0:T(8,128)S(1)})) conditional(s32[]{:T(128)} %bitcast.154, (s32[256]{0:T(256)S(1)}, s32[256]{0:T(256)S(1)}, s32[]{:T(128)}, bf16[3,1024,12,64]{1,3,2,0:T(8,128)(2,1)}, bf16[3,256,12,64]{1,3,2,0:T(8,128)(2,1)S(1)}, /*index=5*/f32[3,1024,12]{1,2,0:T(8,128)}, ...), branch_computations={%region_18.18_spmd, %region_19.19_spmd} | conditional | flops 1228079104 | bytes 45321288 | solution.py:122
  661.6 6.4 fusion.39
  670.2 8.5 bitcast_add_fusion.1
  678.6 6.1 bitcast_add_fusion
  702.3 7.2 fusion.76
  712.7 25.8 %all-reduce.17 = (bf16[768]{0:T(1024)(128)(2,1)}, bf16[768]{0:T(1024)(128)(2,1)}, bf16[768]{0:T(1024)(128)(2,1)}, bf16[768]{0:T(1024)(128)(2,1)}, bf16[768]{0:T(...) all-reduce(bf16[768]{0:T(1024)(128)(2,1)} %copy-done.57, ...), channel_id=1, replica_groups=mesh['ctx'=4,'fsdp'=8] {'fsdp'}, use_global_device_ids=true, to_apply=%add.7 | all-reduce | flops 9984 | bytes 39936
  751.1 9.2 %all-reduce.19 = (bf16[96]{0:T(256)(128)(2,1)}, bf16[96]{0:T(256)(128)(2,1)}, bf16[96]{0:T(256)(128)(2,1)}, bf16[96]{0:T(256)(128)(2,1)}, bf16[96]{0:T(256)(128)...) all-reduce(bf16[96]{0:T(256)(128)(2,1)} %dynamic-slice.9, ...), channel_id=1, replica_groups=mesh['ctx'=4,'fsdp'=8] {'ctx'}, use_global_device_ids=true, to_apply=%region_25.26 | all-reduce | flops 1152 | bytes 4608 | tf_op jit(solution)/shard_map/psum | solution.py:391
  770.8 9.0 %reduce-scatter.5.cloned.1.call-done = bf16[96,2304]{1,0:T(8,128)(2,1)} async-done(((bf16[768,2304]{1,0:T(8,128)(2,1)}), bf16[96,2304]{1,0:T(8,128)(2,1)}) %reduce-scatter.5.cloned.1.call-update) | async-done | bytes 442384 | tf_op jit(solution)/shard_map/reduce_scatter | solution.py:356
  784.8 8.8 %add_convert_fusion.2 = bf16[768,768]{1,0:T(8,128)(2,1)} fusion(f32[768,768]{1,0:T(8,128)S(1)} %copy-done.19, bf16[768,3072]{1,0:T(8,128)(2,1)} %multiply_convert_fusion.4, bf16[3072,768]{1,0:T(8,128)(2,1)} %all-gather.20.cloned.1.call-done, f32[768]{0:T(1024)S(1)} %copy-done.60), kind=kOutput, calls=%fused_computation.111 | convolution fusion | flops 3625648128 | bytes 12979200 | tf_op jit(solution)/shard_map/dot_general | solution.py:240
  793.6 65.6 %all-reduce.23.cloned.1.call-done = (bf16[96,2304]{1,0:T(8,128)(2,1)}, bf16[96,768]{1,0:T(8,128)(2,1)}, bf16[96,3072]{1,0:T(8,128)(2,1)}, bf16[384,768]{1,0:T(8,128)(2,1)}) async-done(((bf16[96,2304]{1,0:T(8,128)(2,1)}, bf16[96,768]{1,0:T(8,128)(2,1)}, bf16[96,3072]{1,0:T(8,128)(2,1)}, bf16[384,768]{1,0:T(8,128)(2,1)}), (bf16[96,2304]{1,0:T(8,128)(2,1)}, bf16[96,768]{1,0:T(8,128)(2,1)}, ...) | async-done | bytes 1769488 | tf_op jit(solution)/shard_map/psum | solution.py:391
  (333 shorter events, 169.4 us)
Async XLA Ops:
  7.2 36.2 %copy-start.3 = (bf16[3,256,768]{2,1,0:T(8,128)(2,1)S(1)}, bf16[3,256,768]{2,1,0:T(8,128)(2,1)}, u32[]{:S(2)}) copy-start(bf16[3,256,768]{2,1,0:T(8,128)(2,1)} %param.27) | copy-start | bytes 3538948
  7.2 39.6 %all-gather.10.cloned.1.call-start = ((), (), s32[]{:S(2)}) async-start(), calls=%async_computation.4 | async-start | bytes 3981312 | tf_op jit(solution)/shard_map/all_gather | solution.py:170
  7.9 137.5 %all-gather.12.cloned.1.call-start = ((), (), s32[]{:S(2)}) async-start(), calls=%async_computation.5 | async-start | bytes 5898240 | tf_op jit(solution)/shard_map/all_gather | solution.py:208
  43.4 8.3 copy-start.40
  54.7 5.3 copy-start.15
  56.2 178.7 %all-gather.14.cloned.1.call-start = ((), (), s32[]{:S(2)}) async-start(), calls=%async_computation.6 | async-start | bytes 5898240 | tf_op jit(solution)/shard_map/all_gather | solution.py:209
  60.0 5.1 copy-start.61
  60.0 13.9 %copy-start.22 = (bf16[768,768]{1,0:T(8,128)(2,1)S(1)}, bf16[768,768]{1,0:T(8,128)(2,1)}, u32[]{:S(2)}) copy-start(bf16[768,768]{1,0:T(8,128)(2,1)} %get-tuple-element.1039) | copy-start | bytes 3538948
  61.5 197.4 %all-gather.16.cloned.1.call-start = ((), (), s32[]{:S(2)}) async-start(), calls=%async_computation.7 | async-start | bytes 1327104 | tf_op jit(solution)/shard_map/all_gather | solution.py:173
  62.1 237.5 %all-gather.18.cloned.1.call-start = ((), (), s32[]{:S(2)}) async-start(), calls=%async_computation.8 | async-start | bytes 5308416 | tf_op jit(solution)/shard_map/all_gather | solution.py:177
  62.7 277.6 %all-gather.20.cloned.1.call-start = ((), (), s32[]{:S(2)}) async-start(), calls=%async_computation.9 | async-start | bytes 5308416 | tf_op jit(solution)/shard_map/all_gather | solution.py:179
  63.3 499.9 %all-gather.22.cloned.1.call-start = ((), (), s32[]{:S(2)}) async-start(), calls=%async_computation.10 | async-start | bytes 7864320 | tf_op jit(solution)/shard_map/all_gather | solution.py:315
  78.2 496.3 %all-gather.24.cloned.1.call-start = ((), (), s32[]{:S(2)}) async-start(), calls=%async_computation.11 | async-start | bytes 7864320 | tf_op jit(solution)/shard_map/all_gather | solution.py:316
  251.5 5.1 copy-start
  251.5 5.1 copy-start.11
  251.5 5.1 copy-start.23
  251.5 5.1 copy-start.35
  251.6 5.1 copy-start.29
  261.9 37.8 %copy-start.53 = (f32[768]{0:T(1024)S(1)}, f32[768]{0:T(1024)}, u32[]{:S(2)}) copy-start(f32[768]{0:T(1024)} %convert_element_type.292) | copy-start | bytes 9220
  261.9 37.7 %copy-start.58 = (f32[768]{0:T(1024)S(1)}, f32[768]{0:T(1024)}, u32[]{:S(2)}) copy-start(f32[768]{0:T(1024)} %convert_element_type.293) | copy-start | bytes 9220
  261.9 112.8 %copy-start.46 = (f32[768]{0:T(1024)}, f32[768]{0:T(1024)S(1)}, u32[]{:S(2)}) copy-start(f32[768]{0:T(1024)S(1)} %broadcast_multiply_fusion) | copy-start | bytes 9220
  263.9 46.5 %copy-start.55 = (f32[768]{0:T(1024)}, f32[768]{0:T(1024)S(1)}, u32[]{:S(2)}) copy-start(f32[768]{0:T(1024)S(1)} %fusion.72) | copy-start | bytes 9220
  263.9 76.4 %copy-start.13 = (bf16[3,256,768]{2,1,0:T(8,128)(2,1)S(1)}, bf16[3,256,768]{2,1,0:T(8,128)(2,1)}, u32[]{:S(2)}) copy-start(bf16[3,256,768]{2,1,0:T(8,128)(2,1)} %param.41) | copy-start | bytes 3538948
  340.3 29.5 %copy-start.18 = (f32[768,768]{1,0:T(8,128)S(1)}, f32[768,768]{1,0:T(8,128)}, u32[]{:S(2)}) copy-start(f32[768,768]{1,0:T(8,128)} %copy-done.17) | copy-start | bytes 7077892
  340.3 29.5 %copy-start.54 = (f32[768]{0:T(1024)S(1)}, f32[768]{0:T(1024)}, u32[]{:S(2)}) copy-start(f32[768]{0:T(1024)} %convert_element_type.292) | copy-start | bytes 9220
  340.3 29.5 %copy-start.56 = (f32[768]{0:T(1024)S(1)}, f32[768]{0:T(1024)}, u32[]{:S(2)}) copy-start(f32[768]{0:T(1024)} %copy-done.55) | copy-start | bytes 9220
  340.3 29.5 %copy-start.62 = (bf16[768,3072]{1,0:T(8,128)(2,1)S(1)}, bf16[768,3072]{1,0:T(8,128)(2,1)}, u32[]{:S(2)}) copy-start(bf16[768,3072]{1,0:T(8,128)(2,1)} %all-gather.18.cloned.1.call-done) | copy-start | bytes 14155780
  369.8 4.9 copy-start.65
  369.8 4.8 copy-start.49
  386.3 384.5 %reduce-scatter.7.cloned.1.call-start = ((), (), s32[]{:S(2)}) async-start(), calls=%async_computation.13 | async-start | bytes 1327104 | tf_op jit(solution)/shard_map/reduce_scatter | solution.py:365
  390.1 380.7 %reduce-scatter.9.cloned.1.call-start = ((), (), s32[]{:S(2)}) async-start(), calls=%async_computation.14 | async-start | bytes 5308416 | tf_op jit(solution)/shard_map/reduce_scatter | solution.py:377
  398.5 372.4 %reduce-scatter.11.cloned.1.call-start = ((), (), s32[]{:S(2)}) async-start(), calls=%async_computation.15 | async-start | bytes 5308416 | tf_op jit(solution)/shard_map/reduce_scatter | solution.py:383
  417.5 362.3 %reduce-scatter.5.cloned.1.call-start = ((), (), s32[]{:S(2)}) async-start(), calls=%async_computation.12 | async-start | bytes 3981312 | tf_op jit(solution)/shard_map/reduce_scatter | solution.py:356
  428.9 4.7 copy-start.5
  435.7 5.1 copy-start.1
  435.7 5.1 copy-start.36
  465.2 77.0 %copy-start.32 = (f32[3,12,256]{2,0,1:T(4,128)S(1)}, f32[3,12,256]{2,0,1:T(4,128)}, u32[]{:S(2)}) copy-start(f32[3,12,256]{2,0,1:T(4,128)} %copy-done.31) | copy-start | bytes 110596
  696.9 5.3 copy-start.4
  696.9 5.3 copy-start.39
  696.9 5.3 copy-start.41
  697.0 162.3 %all-reduce.23.cloned.1.call-start = ((), (), s32[]{:S(2)}) async-start(), calls=%async_computation.16 | async-start | bytes 3538944 | tf_op jit(solution)/shard_map/psum | solution.py:391
  700.9 8.5 copy-start.57
  702.2 7.2 copy-start.51
  702.2 8.6 copy-start.43
  710.9 69.6 %copy-start.7 = (f32[768,768]{1,0:T(8,128)S(1)}, f32[768,768]{1,0:T(8,128)}, u32[]{:S(2)}) copy-start(f32[768,768]{1,0:T(8,128)} %copy-done.6) | copy-start | bytes 7077892
  710.9 69.6 %copy-start.45 = (f32[768]{0:T(1024)S(1)}, f32[768]{0:T(1024)}, u32[]{:S(2)}) copy-start(f32[768]{0:T(1024)} %copy-done.44) | copy-start | bytes 9220
  780.5 4.2 copy-start.19
  859.3 5.9 copy-start.28
  (31 other events, 65.6 us)
Sparse Core Ops, SparseCore 0:
  9.9 36.8 all-gather.9
  56.3 89.0 all-gather.11
  147.6 87.3 all-gather.13
  236.6 22.2 all-gather.15
  260.7 38.9 all-gather.17
  301.4 38.9 all-gather.19
  341.9 114.8 all-gather.21
  458.3 116.1 all-gather.23
  577.7 34.9 reduce-scatter.6
  616.5 53.8 reduce-scatter.8
  673.8 54.2 reduce-scatter.10
  731.9 47.8 reduce-scatter.4
  782.6 76.5 all-reduce.22
where the time goes:
time: 881 us; the launch traced here: 873 us
  waiting for transfers between devices  306 us (35%)
  matrix products  197 us (22%)
  blocking collectives  165 us (19%)
  local copies, waits for them, and re-layouts  111 us (13%)
  other arithmetic  65.2 us (7%)
  between operations  16.8 us (2%)
  loops' own time  11.5 us (1%)
    all_gather x1, waiting for transfers between devices, local(): lax.all_gather(values_seq, 'ctx', axis=1, tiled=True)  89.5 us
    all_gather x1, blocking collectives, local(): lax.all_gather(jnp.transpose(row_stats, (0, 2, 1)).astype(jnp.bfloat16),...  75 us
    all_gather x1, waiting for transfers between devices, local(): lax.all_gather(keys_seq, 'ctx', axis=1, tiled=True)  67 us
    psum x1, waiting for transfers between devices, local(): lax.psum(as_sent(tuple(summed)), 'ctx')  65.6 us
    unnamed x2, blocking collectives  51.8 us
    all_gather x1, waiting for transfers between devices, local(): lax.all_gather(up_projection_weight, 'fsdp', axis=0, tiled=True)  35.7 us
    unnamed x161, local copies, waits for them, and re-layouts  35.6 us
    dot_general x4, matrix products, key_update(): jnp.einsum('shbn,sbhe->snhe', score_grad, query_blk, preferred_element_ty...  35.2 us
  transfers between devices with their start and end apart: 13, of which 9 were waited for; matrix products, arithmetic and copies ran while one was open for 39% of the time, Pallas kernels for 0%

commit v1 on v0

--- a/solution.py
+++ b/solution.py
@@ -3,6 +3,8 @@
 import jax
 import jax.numpy as jnp
 from jax import lax
+from jax.experimental import pallas as pl
+from jax.experimental.pallas import tpu as pltpu
 from jax.sharding import PartitionSpec as P
 
 HEADS = 12
@@ -133,7 +135,7 @@
     return lax.fori_loop(0, block_count, one_block, carry_state)
 
 
-def local(
+def local_general(
     hidden_in,
     attn_gain,
     attn_shift,
@@ -393,7 +395,405 @@
     return (block_out, input_grad) + tuple(summed) + (row_stats,)
 
 
+ROWS = 256
+
+
+def low(value):
+    return value.astype(jnp.bfloat16)
+
+
+def wide(value):
+    return value.astype(jnp.float32)
+
+
+def dot(a, b):
+    return jnp.dot(a, b, preferred_element_type=jnp.float32)
+
+
+def xor_send(value, axis, bit, count):
+    return lax.ppermute(value, axis, [(i, i ^ bit) for i in range(count)])
+
+
+def shift_send(value, steps, count):
+    return lax.ppermute(value, "ctx", [(i, (i + steps) % count) for i in range(count)])
+
+
+def gather_fsdp(piece):
+    me = lax.axis_index("fsdp")
+    rows = piece.shape[0]
+    half = rows // 2
+    by_x = xor_send(piece, "fsdp", 2, 8)
+    by_y = xor_send(piece, "fsdp", 4, 8)
+    corner_top = xor_send(by_x[:half], "fsdp", 4, 8)
+    corner_low = xor_send(by_y[half:], "fsdp", 2, 8)
+    parts = [(0, 0, piece), (2, 0, by_x), (4, 0, by_y), (6, 0, corner_top), (6, half, corner_low)]
+    whole = jnp.zeros((8 * rows,) + piece.shape[1:], piece.dtype)
+    for place, offset, part in parts:
+        other = xor_send(part, "fsdp", 1, 8)
+        start = jnp.bitwise_xor(me, place) * rows + offset
+        whole = lax.dynamic_update_slice_in_dim(whole, part, start, 0)
+        start = jnp.bitwise_xor(me, place + 1) * rows + offset
+        whole = lax.dynamic_update_slice_in_dim(whole, other, start, 0)
+    return whole
+
+
+def scatter_fsdp(grad):
+    me = lax.axis_index("fsdp")
+    core, x, y = me % 2, (me // 2) % 2, me // 4
+    rows, columns = grad.shape
+    blocks = grad.reshape(2, 2, 2, rows // 8, columns)
+    kept = lax.dynamic_index_in_dim(blocks, core, 2, keepdims=False)
+    sent = low(lax.dynamic_index_in_dim(blocks, 1 - core, 2, keepdims=False))
+    total = low(wide(kept) + wide(xor_send(sent, "fsdp", 1, 8)))
+    half = rows // 16
+    top, bottom = total[:, :, :half], total[:, :, half:]
+
+    def fold(part, axis, place, bit):
+        keep = lax.dynamic_index_in_dim(part, place, axis, keepdims=False)
+        send = lax.dynamic_index_in_dim(part, 1 - place, axis, keepdims=False)
+        return low(wide(keep) + wide(xor_send(send, "fsdp", bit, 8)))
+
+    top = fold(fold(top, 1, x, 2), 0, y, 4)
+    bottom = fold(fold(bottom, 0, y, 4), 0, x, 2)
+    return jnp.concatenate([top, bottom], axis=0)
+
+
+def sum_ctx(part):
+    me = lax.axis_index("ctx")
+    odd = me % 2
+    rows = part.shape[0]
+    halves = part.reshape((2, rows // 2) + part.shape[1:])
+    keep = lax.dynamic_index_in_dim(halves, odd, 0, keepdims=False)
+    send = lax.dynamic_index_in_dim(halves, 1 - odd, 0, keepdims=False)
+    own = low(wide(keep) + wide(xor_send(send, "ctx", 1, 4)))
+    own = low(wide(own) + wide(xor_send(own, "ctx", 2, 4)))
+    other = xor_send(own, "ctx", 1, 4)
+    return jnp.where(odd == 0, jnp.concatenate([own, other]), jnp.concatenate([other, own]))
+
+
+def gather_ctx(block):
+    me = lax.axis_index("ctx")
+    whole = jnp.zeros((4,) + block.shape, block.dtype)
+    whole = lax.dynamic_update_index_in_dim(whole, block, me, 0)
+    right = left = block
+    for step in range(1, 4):
+        right = lax.ppermute(right, "ctx", [(i, i + 1) for i in range(step - 1, 3)])
+        left = lax.ppermute(left, "ctx", [(i, i - 1) for i in range(1, 5 - step)])
+        source = (me - step) % 4
+        other = (me + step) % 4
+        whole = lax.dynamic_update_index_in_dim(
+            whole,
+            jnp.where(me >= step, right, lax.dynamic_index_in_dim(whole, source, 0, keepdims=False)),
+            source,
+            0,
+        )
+        whole = lax.dynamic_update_index_in_dim(
+            whole,
+            jnp.where(me + step < 4, left, lax.dynamic_index_in_dim(whole, other, 0, keepdims=False)),
+            other,
+            0,
+        )
+    return whole.reshape((-1,) + block.shape[1:])
+
+
+def scatter_ctx(total):
+    me = lax.axis_index("ctx")
+
+    def block(index):
+        return lax.dynamic_index_in_dim(total, jnp.clip(index, 0, 3), 0, keepdims=False)
+
+    right = left = None
+    for step in range(3):
+        going_right, going_left = block(3 - step + me), block(step - 3 + me)
+        if step:
+            going_right = wide(going_right) + wide(right)
+            going_left = wide(going_left) + wide(left)
+        right = lax.ppermute(low(going_right), "ctx", [(i, i + 1) for i in range(step + 1)])
+        left = lax.ppermute(low(going_left), "ctx", [(i, i - 1) for i in range(3 - step, 4)])
+    return wide(block(me)) + wide(right) + wide(left)
+
+
+def heads_to_positions(value, ordered_axis):
+    me = lax.axis_index("ctx")
+    result = jnp.zeros(value.shape, value.dtype)
+    result = lax.dynamic_update_index_in_dim(
+        result, lax.dynamic_index_in_dim(value, me, 0, keepdims=False), me, 0
+    )
+    for step in (2, 1, 3):
+        piece = lax.dynamic_index_in_dim(value, (me + step) % 4, 0, keepdims=False)
+        result = lax.dynamic_update_index_in_dim(
+            result, shift_send(piece, step, 4), (me - step) % 4, 0
+        )
+    return jnp.moveaxis(result, 0, ordered_axis)
+
+
+def masked_scores(keys, queries_t, tile):
+    scores = dot(keys, queries_t)
+    key_pos = lax.broadcasted_iota(jnp.int32, (ROWS, ROWS), 0)
+    query_pos = lax.broadcasted_iota(jnp.int32, (ROWS, ROWS), 1)
+    diagonal = jnp.where(key_pos <= query_pos, scores[tile * ROWS :], NEG_BIG)
+    if tile == 0:
+        return diagonal
+    return jnp.concatenate([scores[: tile * ROWS], diagonal], axis=0)
+
+
+def attend_kernel(qkv_ref, out_ref, stats_ref):
+    length, width = out_ref.shape
+    heads = width // HD
+    queries_t = qkv_ref[:, :width].T
+    values_t = qkv_ref[:, 2 * width :].T
+    for head in range(heads):
+        keys = qkv_ref[:, width + head * HD : width + (head + 1) * HD]
+        lanes = slice(head * HD, (head + 1) * HD)
+        for tile in range(length // ROWS):
+            rows = slice(tile * ROWS, (tile + 1) * ROWS)
+            seen = (tile + 1) * ROWS
+            scores = masked_scores(keys[:seen], queries_t[lanes, rows], tile)
+            top = jnp.max(scores, axis=0, keepdims=True)
+            weights = jnp.exp(scores - top)
+            total = jnp.sum(weights, axis=0, keepdims=True)
+            mixed = dot(values_t[lanes, :seen], low(weights)) / total
+            out_ref[rows, lanes] = mixed.T
+            stats_ref[head : head + 1, rows] = top + jnp.log(total)
+
+
+def attend_back_kernel(qkv_ref, att_ref, grad_ref, stats_ref, out_ref, key_ref, value_ref):
+    length, width = att_ref.shape
+    heads = width // HD
+    queries_t = qkv_ref[:, :width].T
+    keys_t = qkv_ref[:, width : 2 * width].T
+    grad_t = grad_ref[...].T
+    product_t = (att_ref[...] * wide(grad_ref[...])).T
+    for head in range(heads):
+        lanes = slice(head * HD, (head + 1) * HD)
+        queries = qkv_ref[:, head * HD : (head + 1) * HD]
+        keys = qkv_ref[:, width + head * HD : width + (head + 1) * HD]
+        values = qkv_ref[:, 2 * width + head * HD : 2 * width + (head + 1) * HD]
+        grads = grad_ref[:, lanes]
+        delta = jnp.sum(product_t[lanes], axis=0, keepdims=True)
+        key_ref[...] = jnp.zeros_like(key_ref)
+        value_ref[...] = jnp.zeros_like(value_ref)
+        for tile in range(length // ROWS):
+            rows = slice(tile * ROWS, (tile + 1) * ROWS)
+            seen = (tile + 1) * ROWS
+            scores = masked_scores(keys[:seen], queries_t[lanes, rows], tile)
+            prob = jnp.exp(scores - stats_ref[head : head + 1, rows])
+            prob_grad = dot(values[:seen], grad_t[lanes, rows])
+            score_grad = low(prob * (prob_grad - delta[:, rows]))
+            query_grad = dot(keys_t[lanes, :seen], score_grad)
+            out_ref[rows, lanes] = low(low(query_grad).T * jnp.bfloat16(0.125))
+            key_ref[:seen] += dot(score_grad, queries[rows])
+            value_ref[:seen] += dot(low(prob), grads[rows])
+        out_ref[:, width + head * HD : width + (head + 1) * HD] = low(key_ref[...])
+        out_ref[:, 2 * width + head * HD : 2 * width + (head + 1) * HD] = low(value_ref[...])
+
+
+def attend(qkv):
+    length, width = qkv.shape[0], qkv.shape[1] // 3
+    return pl.pallas_call(
+        attend_kernel,
+        out_shape=(
+            jax.ShapeDtypeStruct((length, width), jnp.float32),
+            jax.ShapeDtypeStruct((width // HD, length), jnp.float32),
+        ),
+        compiler_params=pltpu.CompilerParams(vmem_limit_bytes=40 * 1024 * 1024),
+        cost_estimate=pl.CostEstimate(
+            flops=8 * length * length * width, bytes_accessed=4 * length * width * 4, transcendentals=2 * length * length
+        ),
+    )(qkv)
+
+
+def attend_back(qkv, attended, grads, stats):
+    length, width = attended.shape
+    return pl.pallas_call(
+        attend_back_kernel,
+        out_shape=jax.ShapeDtypeStruct((length, 3 * width), jnp.bfloat16),
+        scratch_shapes=[pltpu.VMEM((length, HD), jnp.float32), pltpu.VMEM((length, HD), jnp.float32)],
+        compiler_params=pltpu.CompilerParams(vmem_limit_bytes=40 * 1024 * 1024),
+        cost_estimate=pl.CostEstimate(
+            flops=20 * length * length * width, bytes_accessed=5 * length * width * 4, transcendentals=2 * length * length
+        ),
+    )(qkv, attended, grads, stats)
+
+
+def norm_parts(values):
+    center = values - jnp.mean(values, axis=-1, keepdims=True)
+    inverse = lax.rsqrt(jnp.mean(center * center, axis=-1, keepdims=True) + 1e-05)
+    return center * inverse, inverse
+
+
+def norm_back(grad, unit, inverse, gain):
+    inner = grad * gain
+    mean_inner = jnp.mean(inner, axis=-1, keepdims=True)
+    mean_product = jnp.mean(inner * unit, axis=-1, keepdims=True)
+    return (
+        inverse * (inner - mean_inner - unit * mean_product),
+        jnp.sum(grad * unit, axis=0),
+        jnp.sum(grad, axis=0),
+    )
+
+
+def local_fast(
+    hidden_in,
+    attn_gain,
+    attn_shift,
+    query_key_value_weight,
+    query_bias,
+    value_bias,
+    projection_output_weight,
+    projection_output_bias,
+    mlp_gain,
+    mlp_shift,
+    up_projection_weight,
+    up_projection_bias,
+    down_projection_weight,
+    down_projection_bias,
+    out_grad,
+):
+    seqs, block_rows, width = hidden_in.shape
+    place = lax.axis_index("ctx")
+    share = width // 4
+    row_count = seqs * block_rows
+    shard = width // 8
+
+    vectors = jnp.stack(
+        [attn_gain, attn_shift, query_bias, value_bias, projection_output_bias, mlp_gain, mlp_shift, down_projection_bias]
+        + list(up_projection_bias.reshape(4, shard))
+        + [attn_gain] * 4
+    )
+    vectors_all = wide(gather_fsdp(vectors)).reshape(8, 16, shard)
+    (gain_1, shift_1, bias_q, bias_v, bias_proj, gain_2, shift_2, bias_down) = (
+        vectors_all[:, i].reshape(width) for i in range(8)
+    )
+    bias_up = vectors_all[:, 8:12].reshape(4 * width)
+
+    def heads_here(array):
+        return lax.dynamic_slice_in_dim(array, place * share, share, array.ndim - 1)
+
+    qkv_own = heads_here(query_key_value_weight.reshape(shard, 3, width)).reshape(shard, 3 * share)
+    qkv_all = gather_fsdp(qkv_own)
+    full = [gather_ctx(hidden_in[s]) for s in range(seqs)]
+    proj_all = gather_fsdp(projection_output_weight)
+    up_all = gather_fsdp(up_projection_weight)
+    down_all = gather_fsdp(down_projection_weight)
+
+    bias_qkv = jnp.concatenate([heads_here(bias_q), jnp.zeros((share,), jnp.float32), heads_here(bias_v)])
+    scale = jnp.concatenate([jnp.full((share,), 0.125, jnp.float32), jnp.ones((2 * share,), jnp.float32)])
+    normed, qkv, attended, stats, gathered = [], [], [], [], []
+    for s in range(seqs):
+        unit, unused = norm_parts(wide(full[s]))
+        normed.append(low(unit * gain_1 + shift_1))
+        qkv.append(low((dot(normed[s], qkv_all) + bias_qkv) * scale))
+        att, stat = attend(qkv[s])
+        attended.append(att)
+        stats.append(stat)
+        gathered.append(heads_to_positions(low(att).reshape(4, block_rows, share), 1).reshape(block_rows, width))
+    stats_all = jnp.stack(stats)
+    heads_each = stats_all.shape[1]
+    stats_out = heads_to_positions(
+        jnp.moveaxis(stats_all.reshape(seqs, heads_each, 4, block_rows), 2, 0), 1
+    ).reshape(seqs, 4 * heads_each, block_rows)
+    attended_low = jnp.concatenate(gathered)
+
+    hidden = wide(hidden_in).reshape(row_count, width)
+    middle = hidden + dot(attended_low, proj_all) + bias_proj
+    unit_2, inverse_2 = norm_parts(middle)
+    second = low(unit_2 * gain_2 + shift_2)
+    inner = dot(second, up_all) + bias_up
+    below = 0.5 * (1.0 + lax.erf(inner * 0.7071067811865476))
+    active = low(inner * below)
+    slope = below + inner * (jnp.exp(-0.5 * inner * inner) * 0.3989422804014327)
+    block_out = low(middle + dot(active, down_all) + bias_down).reshape(seqs, block_rows, width)
+
+    branch_down = out_grad.reshape(row_count, width)
+    top = wide(branch_down)
+    contract_rows = (((0,), (0,)), ((), ()))
+    contract_columns = (((1,), (1,)), ((), ()))
+
+    def weight_grad(a, b):
+        return lax.dot_general(a, b, contract_rows, preferred_element_type=jnp.float32)
+
+    def through(a, b):
+        return lax.dot_general(a, b, contract_columns, preferred_element_type=jnp.float32)
+
+    down_grad = sum_ctx(scatter_fsdp(low(weight_grad(active, branch_down))))
+    inner_grad = low(through(branch_down, down_all) * slope)
+    up_grad = sum_ctx(scatter_fsdp(low(weight_grad(second, inner_grad))))
+    grad_middle, gain_2_grad, shift_2_grad = norm_back(through(inner_grad, up_all), unit_2, inverse_2, gain_2)
+    grad_middle = grad_middle + top
+    branch_up = low(grad_middle)
+    att_grad = low(through(branch_up, proj_all))
+    proj_grad = sum_ctx(scatter_fsdp(low(weight_grad(attended_low, branch_up))))
+
+    att_grad = jnp.moveaxis(att_grad.reshape(seqs, block_rows, 4, share), 2, 1)
+    joined, own_grads = [], []
+    qkv_grad = 0.0
+    for s in range(seqs):
+        grads = heads_to_positions(att_grad[s], 0).reshape(4 * block_rows, share)
+        joined.append(attend_back(qkv[s], attended[s], grads, stats[s]))
+        partial_normed = low(through(joined[s], qkv_all)).reshape(4, block_rows, width)
+        own_grads.append(scatter_ctx(partial_normed))
+        qkv_grad = qkv_grad + weight_grad(normed[s], joined[s])
+    qkv_part = scatter_fsdp(low(qkv_grad))
+    pieces = jnp.zeros((4,) + qkv_part.shape, qkv_part.dtype)
+    pieces = lax.dynamic_update_index_in_dim(pieces, qkv_part, place, 0)
+    for step in (2, 1, 3):
+        pieces = lax.dynamic_update_index_in_dim(pieces, shift_send(qkv_part, step, 4), (place - step) % 4, 0)
+    qkv_out = wide(jnp.moveaxis(pieces.reshape(4, shard, 3, share), 0, 2).reshape(shard, 3 * width))
+
+    joined_all = jnp.concatenate(joined)
+    bias_sums = jnp.sum(joined_all, axis=0, dtype=jnp.float32)
+    zero_row = jnp.zeros((width,), jnp.float32)
+    query_bias_grad = lax.dynamic_update_slice_in_dim(zero_row, bias_sums[:share], place * share, 0)
+    value_bias_grad = lax.dynamic_update_slice_in_dim(zero_row, bias_sums[2 * share :], place * share, 0)
+
+    unit_1, inverse_1 = norm_parts(hidden)
+    grad_hidden, gain_1_grad, shift_1_grad = norm_back(jnp.concatenate(own_grads), unit_1, inverse_1, gain_1)
+    input_grad = low(grad_middle + grad_hidden).reshape(seqs, block_rows, width)
+
+    rows = [
+        gain_1_grad,
+        shift_1_grad,
+        query_bias_grad,
+        value_bias_grad,
+        jnp.sum(branch_up, axis=0, dtype=jnp.float32),
+        gain_2_grad,
+        shift_2_grad,
+        jnp.sum(branch_down, axis=0, dtype=jnp.float32),
+    ]
+    up_bias_grad = jnp.sum(inner_grad, axis=0, dtype=jnp.float32)
+    small = jnp.concatenate(
+        [
+            jnp.stack(rows).reshape(8, 8, shard).transpose(1, 0, 2),
+            up_bias_grad.reshape(8, 4, shard),
+            jnp.zeros((8, 4, shard), jnp.float32),
+        ],
+        axis=1,
+    )
+    small = wide(sum_ctx(scatter_fsdp(low(small.reshape(8 * 16, shard)))))
+    return (
+        block_out,
+        input_grad,
+        small[0],
+        small[1],
+        qkv_out,
+        small[2],
+        small[3],
+        wide(proj_grad),
+        small[4],
+        small[5],
+        small[6],
+        wide(up_grad),
+        small[8:12].reshape(4 * shard),
+        wide(down_grad),
+        small[7],
+        stats_out,
+    )
+
+
 def solution(mesh):
+    fast = mesh.shape["ctx"] == 4 and mesh.shape["fsdp"] == 8
+    chosen = local_fast if fast else local_general
     placed = (
         P("fsdp", "ctx", None),
         P("fsdp"),
@@ -412,7 +812,7 @@
         P("fsdp", "ctx", None),
     )
     return jax.shard_map(
-        local,
+        chosen,
         mesh=mesh,
         in_specs=placed,
         out_specs=(

time: 881 us -> 795 us (0.902)
  starting transfers between devices: 0.73 us -> 222 us
  blocking collectives: 165 us -> 0 us
  waiting for transfers between devices: 306 us -> 155 us
  matrix products: 197 us -> 72.5 us
  local copies, waits for them, and re-layouts: 111 us -> 234 us
  Pallas kernels: 0 us -> 36.3 us
  between operations: 16.8 us -> 3.3 us
  loops' own time: 11.5 us -> 0 us
    all_gather x8 -> x0, waiting for transfers between devices: 229 us -> none  [the longest x1 89.5 us: local(): lax.all_gather(values_seq, 'ctx', axis=1, tiled=True)]
    ppermute x0 -> x142, starting transfers between devices: none -> 222 us  [the longest x82 90.2 us: xor_send(): return lax.ppermute(value, axis, [(i, i ^ bit) for i in range(count)])]
    ppermute x0 -> x142, waiting for transfers between devices: none -> 155 us  [the longest x82 86.2 us: xor_send(): return lax.ppermute(value, axis, [(i, i ^ bit) for i in range(count)])]
    dot_general x28 -> x18, matrix products: 197 us -> 72.5 us  [the longest x6 26.3 us: through(): lax.dot_general(a, b, contract_columns, preferred_element_type=jnp.float32)]
    all_gather x3 -> x0, blocking collectives: 104 us -> none  [the longest x1 75 us: local(): lax.all_gather(jnp.transpose(row_stats, (0, 2, 1)).astype(jnp.bfloat16),...]
    dynamic_update_slice x0 -> x89, local copies, waits for them, and re-layouts: none -> 101 us  [the longest x25 44.1 us: gather_fsdp(): whole = lax.dynamic_update_slice_in_dim(whole, part, start, 0)]
    psum x1 -> x0, waiting for transfers between devices: 65.6 us -> none  [local(): lax.psum(as_sent(tuple(summed)), 'ctx')]
    unnamed x2 -> x0, blocking collectives: 51.8 us -> none
  transfers between devices with their start and end apart: 13 -> 142, of which waited for: 9 -> 40; matrix products, arithmetic and copies ran while one was open for 39% -> 37% of each run, Pallas kernels for 0% -> 5%
where the time goes in v1:
time: 795 us; the launch traced here: 782 us
  local copies, waits for them, and re-layouts  234 us (29%)
  starting transfers between devices  222 us (28%)
  waiting for transfers between devices  155 us (19%)
  matrix products  72.5 us (9%)
  other arithmetic  58.9 us (7%)
  Pallas kernels  36.3 us (5%)
    ppermute x82, starting transfers between devices, xor_send(): return lax.ppermute(value, axis, [(i, i ^ bit) for i in range(count)])  90.2 us
    ppermute x82, waiting for transfers between devices, xor_send(): return lax.ppermute(value, axis, [(i, i ^ bit) for i in range(count)])  86.2 us
    dynamic_update_slice x25, local copies, waits for them, and re-layouts, gather_fsdp(): whole = lax.dynamic_update_slice_in_dim(whole, part, start, 0)  44.1 us
    ppermute x9, starting transfers between devices, scatter_ctx(): lax.ppermute(low(going_right), 'ctx', [(i, i + 1) for i in range(step + 1)])  44.1 us
    ppermute x9, waiting for transfers between devices, gather_ctx(): left = lax.ppermute(left, 'ctx', [(i, i - 1) for i in range(1, 5 - step)])  41.7 us
    ppermute x24, starting transfers between devices, shift_send(): lax.ppermute(value, 'ctx', [(i, (i + steps) % count) for i in range(count)])  37.3 us
    dynamic_update_slice x25, local copies, waits for them, and re-layouts, gather_fsdp(): whole = lax.dynamic_update_slice_in_dim(whole, other, start, 0)  36.3 us
    dot_general x6, matrix products, through(): lax.dot_general(a, b, contract_columns, preferred_element_type=jnp.float32)  26.3 us
  transfers between devices with their start and end apart: 142, of which 40 were waited for; matrix products, arithmetic and copies ran while one was open for 37% of the time, Pallas kernels for 5%

profile of v1, /device:TPU:0, one launch (start us, length us, event | category | flops | bytes accessed | tf_op | source)
XLA Modules:
  0.0 781.9 jit_solution(6297962437453648804)
XLA Ops:
  75.0 3.6 dynamic_update_slice.339
  78.6 3.6 dynamic_update_slice.340
  89.6 4.4 collective-permute-start
  102.1 3.7 dynamic_update_slice.343
  109.4 5.3 collective-permute-start.27
  117.7 3.7 dynamic_update_slice.346
  137.2 6.2 collective-permute-start.36
  144.0 6.2 collective-permute-start.37
  157.6 4.3 collective-permute-done.37
  172.4 8.3 %collective-permute-done.64 = bf16[384,768]{1,0:T(8,128)(2,1)} collective-permute-done((bf16[384,768]{1,0:T(8,128)(2,1)S(1)}, bf16[384,768]{1,0:T(8,128)(2,1)}, u32[]{:S(2)}, u32[]{:S(2)}) %collective-permute-start.64) | collective-permute-done | bytes 589856 | tf_op jit(solution)/shard_map/ppermute | solution.py:414
  195.9 7.7 collective-permute-done.30
  206.0 5.3 collective-permute-done.39
  213.7 9.4 %collective-permute-done.5 = bf16[256,768]{1,0:T(8,128)(2,1)S(1)} collective-permute-done((bf16[256,768]{1,0:T(8,128)(2,1)S(1)}, bf16[256,768]{1,0:T(8,128)(2,1)S(1)}, u32[]{:S(2)}, u32[]{:S(2)}) %collective-permute-start.5) | collective-permute-done | bytes 393248 | tf_op jit(solution)/shard_map/ppermute | solution.py:481
  226.2 7.7 collective-permute-done.32
  236.5 7.3 collective-permute-done.41
  249.8 5.2 shard_map.272
  257.3 5.2 shard_map.271
  265.3 5.2 shard_map.270
  293.6 3.8 collective-permute-start.44
  312.3 4.0 collective-permute-done.140
  320.6 3.8 collective-permute-start.35
  339.5 7.1 multiply_convert_fusion
  346.7 8.6 %fusion.116 = (bf16[3072]{0:T(1024)(128)(2,1)S(1)}, bf16[768,3072]{1,0:T(8,128)(2,1)S(1)}) fusion(f32[768,3072]{1,0:T(8,128)S(1)} %get-tuple-element.170, f32[3072]{0:T(1024)S(1)} %copy-done.70, bf16[3072,768]{1,0:T(8,128)(2,1)} %constant_dynamic-update-slice_fusion.8, bf16[768,768]{1,0:T(8,128)(2,1)S(1)} %bitcast.638), kind=kOutput, calls=%fused_computation.467 | convolution fusion | flops 3652187136 | bytes 20072448 | tf_op jit(solution)/shard_map/dot_general | solution.py:717
  355.2 6.8 multiply_reduce_fusion.3
  369.5 6.5 convolution_convert_fusion.1
  376.0 5.9 convolution_convert_fusion
  381.9 7.2 add_convert_fusion
  430.2 6.8 shard_map.275
  439.6 3.9 collective-permute-start.74
  447.0 6.8 shard_map.274
  461.9 7.0 shard_map.273
  471.5 7.6 convert_reduce_fusion
  491.2 4.1 add_convert_fusion.2
  507.1 6.1 collective-permute-done.75
  524.4 3.8 collective-permute-done.111
  585.9 7.2 collective-permute-done.121
  595.2 5.3 collective-permute-start.88
  613.0 24.5 %collective-permute-start.77 = (bf16[256,768]{1,0:T(8,128)(2,1)S(1)}, bf16[256,768]{1,0:T(8,128)(2,1)S(1)}, u32[]{:S(2)}, u32[]{:S(2)}) collective-permute-start(bf16[256,768]{1,0:T(8,128)(2,1)S(1)} %get-tuple-element.88), channel_id=1, source_target_pairs={{0,8},{8,16},{16,24},{1,9},{9,17},{17,25},{2,10},{10,18},{18,26},{... | collective-permute-start | bytes 1179656 | tf_op jit(solution)/shard_map/ppermute | solution.py:511
  642.8 7.1 collective-permute-done.80
  678.6 7.2 collective-permute-start.104
  707.8 7.0 collective-permute-done.126
  717.3 7.6 collective-permute-done.134
  731.9 4.1 collective-permute-done.135
  736.2 4.5 collective-permute-start.136
  743.6 12.6 %collective-permute-done.136 = bf16[192,768]{1,0:T(8,128)(2,1)S(1)} collective-permute-done((bf16[192,768]{1,0:T(8,128)(2,1)S(1)}, bf16[192,768]{1,0:T(8,128)(2,1)S(1)}, u32[]{:S(2)}, u32[]{:S(2)}) %collective-permute-start.136) | collective-permute-done | bytes 294944 | tf_op jit(solution)/shard_map/ppermute | solution.py:414
  756.5 8.3 %collective-permute-start.130 = (bf16[48,3072]{1,0:T(8,128)(2,1)S(1)}, bf16[48,3072]{1,0:T(8,128)(2,1)S(1)}, u32[]{:S(2)}, u32[]{:S(2)}) collective-permute-start(bf16[48,3072]{1,0:T(8,128)(2,1)S(1)} %add_convert_fusion.4), channel_id=1, source_target_pairs={{0,8},{8,0},{16,24},{24,16},{1,9},{9,1},{17,25},{25,17},{2,10},{10... | collective-permute-start | bytes 884744 | tf_op jit(solution)/shard_map/ppermute | solution.py:414
  766.0 5.2 collective-permute-done.137
  775.7 4.9 collective-permute-done.138
  (802 shorter events, 471.1 us)
Async XLA Ops:
  3.2 38.2 %collective-permute-start.6 = (bf16[16,96]{1,0:T(8,128)(2,1)S(1)}, bf16[16,96]{1,0:T(8,128)(2,1)}, u32[]{:S(2)}, u32[]{:S(2)}) collective-permute-start(bf16[16,96]{1,0:T(8,128)(2,1)S(1)} %stack.80), channel_id=1, source_target_pairs={{0,1},{1,0},{2,3},{3,2},{4,5},{5,4},{6,7},{7,6},{8,9},{9,8},{10,11... | collective-permute-start | bytes 9224 | tf_op jit(solution)/shard_map/ppermute | solution.py:414
  3.7 37.9 %collective-permute-start.7 = (bf16[16,96]{1,0:T(8,128)(2,1)S(1)}, bf16[16,96]{1,0:T(8,128)(2,1)}, u32[]{:S(2)}, u32[]{:S(2)}) collective-permute-start(bf16[16,96]{1,0:T(8,128)(2,1)S(1)} %stack.80), channel_id=1, source_target_pairs={{0,2},{1,3},{2,0},{3,1},{4,6},{5,7},{6,4},{7,5},{8,10},{9,11},{10,... | collective-permute-start | bytes 9224 | tf_op jit(solution)/shard_map/ppermute | solution.py:414
  6.3 39.0 %collective-permute-start.9 = (bf16[16,96]{1,0:T(8,128)(2,1)S(1)}, bf16[16,96]{1,0:T(8,128)(2,1)S(1)}, u32[]{:S(2)}, u32[]{:S(2)}) collective-permute-start(bf16[16,96]{1,0:T(8,128)(2,1)S(1)} %stack.80), channel_id=1, source_target_pairs={{0,4},{1,5},{2,6},{3,7},{4,0},{5,1},{6,2},{7,3},{8,12},{9,13},{10,... | collective-permute-start | bytes 9224 | tf_op jit(solution)/shard_map/ppermute | solution.py:414
  7.8 74.5 %collective-permute-start.45 = (bf16[96,768]{1,0:T(8,128)(2,1)}, bf16[96,768]{1,0:T(8,128)(2,1)}, u32[]{:S(2)}, u32[]{:S(2)}) collective-permute-start(bf16[96,768]{1,0:T(8,128)(2,1)} %param.21), channel_id=1, source_target_pairs={{0,1},{1,0},{2,3},{3,2},{4,5},{5,4},{6,7},{7,6},{8,9},{9,8},{10,11... | collective-permute-start | bytes 442376 | tf_op jit(solution)/shard_map/ppermute | solution.py:414
  7.8 74.5 %collective-permute-start.46 = (bf16[96,768]{1,0:T(8,128)(2,1)}, bf16[96,768]{1,0:T(8,128)(2,1)}, u32[]{:S(2)}, u32[]{:S(2)}) collective-permute-start(bf16[96,768]{1,0:T(8,128)(2,1)} %param.21), channel_id=1, source_target_pairs={{0,2},{1,3},{2,0},{3,1},{4,6},{5,7},{6,4},{7,5},{8,10},{9,11},{10,... | collective-permute-start | bytes 442376 | tf_op jit(solution)/shard_map/ppermute | solution.py:414
  41.4 43.0 %collective-permute-start.48 = (bf16[96,768]{1,0:T(8,128)(2,1)}, bf16[96,768]{1,0:T(8,128)(2,1)}, u32[]{:S(2)}, u32[]{:S(2)}) collective-permute-start(bf16[96,768]{1,0:T(8,128)(2,1)} %param.21), channel_id=1, source_target_pairs={{0,4},{1,5},{2,6},{3,7},{4,0},{5,1},{6,2},{7,3},{8,12},{9,13},{10,... | collective-permute-start | bytes 442376 | tf_op jit(solution)/shard_map/ppermute | solution.py:414
  52.4 22.2 %collective-permute-start.15 = (bf16[96,576]{0,1:T(8,128)(2,1)}, bf16[96,576]{0,1:T(8,128)(2,1)}, u32[]{:S(2)}, u32[]{:S(2)}) collective-permute-start(bf16[96,576]{0,1:T(8,128)(2,1)} %bitcast.655), channel_id=1, source_target_pairs={{0,1},{1,0},{2,3},{3,2},{4,5},{5,4},{6,7},{7,6},{8,9},{9,8},{10,11... | collective-permute-start | bytes 331784 | tf_op jit(solution)/shard_map/ppermute | solution.py:414
  82.2 43.8 %collective-permute-start.47 = (bf16[96,768]{1,0:T(8,128)(2,1)}, bf16[96,768]{1,0:T(8,128)(2,1)}, u32[]{:S(2)}, u32[]{:S(2)}) collective-permute-start(bf16[96,768]{1,0:T(8,128)(2,1)} %collective-permute-done.46), channel_id=1, source_target_pairs={{0,1},{1,0},{2,3},{3,2},{4,5},{5,4},{6,7},{7,6},{8,9},{9,8},{10,11... | collective-permute-start | bytes 442376 | tf_op jit(solution)/shard_map/ppermute | solution.py:414
  84.4 25.0 %collective-permute-start.21 = (bf16[48,576]{0,1:T(8,128)(2,1)}, bf16[48,576]{0,1:T(8,128)(2,1)}, u32[]{:S(2)}, u32[]{:S(2)}) collective-permute-start(bf16[48,576]{0,1:T(8,128)(2,1)} %collective-permute-done.20), channel_id=1, source_target_pairs={{0,1},{1,0},{2,3},{3,2},{4,5},{5,4},{6,7},{7,6},{8,9},{9,8},{10,11... | collective-permute-start | bytes 165896 | tf_op jit(solution)/shard_map/ppermute | solution.py:414
  84.8 36.5 %collective-permute-start.23 = (bf16[48,576]{0,1:T(8,128)(2,1)}, bf16[48,576]{0,1:T(8,128)(2,1)}, u32[]{:S(2)}, u32[]{:S(2)}) collective-permute-start(bf16[48,576]{0,1:T(8,128)(2,1)} %collective-permute-done.22), channel_id=1, source_target_pairs={{0,1},{1,0},{2,3},{3,2},{4,5},{5,4},{6,7},{7,6},{8,9},{9,8},{10,11... | collective-permute-start | bytes 165896 | tf_op jit(solution)/shard_map/ppermute | solution.py:414
  89.6 54.5 %collective-permute-start = (bf16[256,768]{1,0:T(8,128)(2,1)}, bf16[256,768]{1,0:T(8,128)(2,1)}, u32[]{:S(2)}, u32[]{:S(2)}) collective-permute-start(bf16[256,768]{1,0:T(8,128)(2,1)} %get-tuple-element.103), channel_id=1, source_target_pairs={{0,8},{8,16},{16,24},{1,9},{9,17},{17,25},{2,10},{10,18},{18,26},{... | collective-permute-start | bytes 1179656 | tf_op jit(solution)/shard_map/ppermute | solution.py:480
  100.8 53.9 %collective-permute-start.1 = (bf16[256,768]{1,0:T(8,128)(2,1)}, bf16[256,768]{1,0:T(8,128)(2,1)}, u32[]{:S(2)}, u32[]{:S(2)}) collective-permute-start(bf16[256,768]{1,0:T(8,128)(2,1)} %get-tuple-element.103), channel_id=1, source_target_pairs={{8,0},{16,8},{24,16},{9,1},{17,9},{25,17},{10,2},{18,10},{26,18},{... | collective-permute-start | bytes 1179656 | tf_op jit(solution)/shard_map/ppermute | solution.py:481
  109.4 41.9 %collective-permute-start.27 = (bf16[256,768]{1,0:T(8,128)(2,1)}, bf16[256,768]{1,0:T(8,128)(2,1)}, u32[]{:S(2)}, u32[]{:S(2)}) collective-permute-start(bf16[256,768]{1,0:T(8,128)(2,1)} %get-tuple-element.104), channel_id=1, source_target_pairs={{0,8},{8,16},{16,24},{1,9},{9,17},{17,25},{2,10},{10,18},{18,26},{... | collective-permute-start | bytes 1179656 | tf_op jit(solution)/shard_map/ppermute | solution.py:480
  134.5 22.9 %collective-permute-start.28 = (bf16[256,768]{1,0:T(8,128)(2,1)}, bf16[256,768]{1,0:T(8,128)(2,1)S(1)}, u32[]{:S(2)}, u32[]{:S(2)}) collective-permute-start(bf16[256,768]{1,0:T(8,128)(2,1)} %get-tuple-element.104), channel_id=1, source_target_pairs={{8,0},{16,8},{24,16},{9,1},{17,9},{25,17},{10,2},{18,10},{26,18},{... | collective-permute-start | bytes 1179656 | tf_op jit(solution)/shard_map/ppermute | solution.py:481
  154.7 32.0 %collective-permute-start.57 = (bf16[96,3072]{1,0:T(8,128)(2,1)S(1)}, bf16[96,3072]{1,0:T(8,128)(2,1)S(1)}, u32[]{:S(2)}, u32[]{:S(2)}) collective-permute-start(bf16[96,3072]{1,0:T(8,128)(2,1)S(1)} %copy-done.47), channel_id=1, source_target_pairs={{0,4},{1,5},{2,6},{3,7},{4,0},{5,1},{6,2},{7,3},{8,12},{9,13},{10,... | collective-permute-start | bytes 1769480 | tf_op jit(solution)/shard_map/ppermute | solution.py:414
  163.5 25.1 %collective-permute-start.66 = (bf16[384,768]{1,0:T(8,128)(2,1)S(1)}, bf16[384,768]{1,0:T(8,128)(2,1)}, u32[]{:S(2)}, u32[]{:S(2)}) collective-permute-start(bf16[384,768]{1,0:T(8,128)(2,1)S(1)} %copy-done.49), channel_id=1, source_target_pairs={{0,4},{1,5},{2,6},{3,7},{4,0},{5,1},{6,2},{7,3},{8,12},{9,13},{10,... | collective-permute-start | bytes 1769480 | tf_op jit(solution)/shard_map/ppermute | solution.py:414
  165.9 25.1 %collective-permute-start.2 = (bf16[256,768]{1,0:T(8,128)(2,1)}, bf16[256,768]{1,0:T(8,128)(2,1)S(1)}, u32[]{:S(2)}, u32[]{:S(2)}) collective-permute-start(bf16[256,768]{1,0:T(8,128)(2,1)} %collective-permute-done), channel_id=1, source_target_pairs={{8,16},{16,24},{9,17},{17,25},{10,18},{18,26},{11,19},{19,27},{12,... | collective-permute-start | bytes 1179656 | tf_op jit(solution)/shard_map/ppermute | solution.py:480
  169.2 25.0 %collective-permute-start.3 = (bf16[256,768]{1,0:T(8,128)(2,1)}, bf16[256,768]{1,0:T(8,128)(2,1)S(1)}, u32[]{:S(2)}, u32[]{:S(2)}) collective-permute-start(bf16[256,768]{1,0:T(8,128)(2,1)} %collective-permute-done.1), channel_id=1, source_target_pairs={{8,0},{16,8},{9,1},{17,9},{10,2},{18,10},{11,3},{19,11},{12,4},{20... | collective-permute-start | bytes 1179656 | tf_op jit(solution)/shard_map/ppermute | solution.py:481
  192.5 89.8 %collective-permute-start.59 = (bf16[48,3072]{1,0:T(8,128)(2,1)}, bf16[48,3072]{1,0:T(8,128)(2,1)}, u32[]{:S(2)}, u32[]{:S(2)}) collective-permute-start(bf16[48,3072]{1,0:T(8,128)(2,1)} %slice.201), channel_id=1, source_target_pairs={{0,4},{1,5},{2,6},{3,7},{4,0},{5,1},{6,2},{7,3},{8,12},{9,13},{10,... | collective-permute-start | bytes 884744 | tf_op jit(solution)/shard_map/ppermute | solution.py:414
  194.2 92.5 %collective-permute-start.61 = (bf16[48,3072]{1,0:T(8,128)(2,1)}, bf16[48,3072]{1,0:T(8,128)(2,1)}, u32[]{:S(2)}, u32[]{:S(2)}) collective-permute-start(bf16[48,3072]{1,0:T(8,128)(2,1)} %slice.202), channel_id=1, source_target_pairs={{0,2},{1,3},{2,0},{3,1},{4,6},{5,7},{6,4},{7,5},{8,10},{9,11},{10,... | collective-permute-start | bytes 884744 | tf_op jit(solution)/shard_map/ppermute | solution.py:414
  203.5 83.4 %collective-permute-start.68 = (bf16[192,768]{1,0:T(8,128)(2,1)}, bf16[192,768]{1,0:T(8,128)(2,1)}, u32[]{:S(2)}, u32[]{:S(2)}) collective-permute-start(bf16[192,768]{1,0:T(8,128)(2,1)} %slice.204), channel_id=1, source_target_pairs={{0,4},{1,5},{2,6},{3,7},{4,0},{5,1},{6,2},{7,3},{8,12},{9,13},{10,... | collective-permute-start | bytes 884744 | tf_op jit(solution)/shard_map/ppermute | solution.py:414
  236.2 36.4 %collective-permute-start.56 = (bf16[96,3072]{1,0:T(8,128)(2,1)}, bf16[96,3072]{1,0:T(8,128)(2,1)}, u32[]{:S(2)}, u32[]{:S(2)}) collective-permute-start(bf16[96,3072]{1,0:T(8,128)(2,1)} %collective-permute-done.55), channel_id=1, source_target_pairs={{0,1},{1,0},{2,3},{3,2},{4,5},{5,4},{6,7},{7,6},{8,9},{9,8},{10,11... | collective-permute-start | bytes 1769480 | tf_op jit(solution)/shard_map/ppermute | solution.py:414
  243.8 32.4 %collective-permute-start.65 = (bf16[384,768]{1,0:T(8,128)(2,1)}, bf16[384,768]{1,0:T(8,128)(2,1)}, u32[]{:S(2)}, u32[]{:S(2)}) collective-permute-start(bf16[384,768]{1,0:T(8,128)(2,1)} %collective-permute-done.64), channel_id=1, source_target_pairs={{0,1},{1,0},{2,3},{3,2},{4,5},{5,4},{6,7},{7,6},{8,9},{9,8},{10,11... | collective-permute-start | bytes 1769480 | tf_op jit(solution)/shard_map/ppermute | solution.py:414
  288.6 32.0 %collective-permute-start.42 = (bf16[256,192]{0,1:T(8,128)(2,1)}, bf16[256,192]{0,1:T(8,128)(2,1)}, u32[]{:S(2)}, u32[]{:S(2)}) collective-permute-start(bf16[256,192]{0,1:T(8,128)(2,1)} %bitcast.664), channel_id=1, source_target_pairs={{0,16},{8,24},{16,0},{24,8},{1,17},{9,25},{17,1},{25,9},{2,18},{10... | collective-permute-start | bytes 294920 | tf_op jit(solution)/shard_map/ppermute | solution.py:418
  292.9 32.5 %collective-permute-start.43 = (bf16[256,192]{0,1:T(8,128)(2,1)}, bf16[256,192]{0,1:T(8,128)(2,1)}, u32[]{:S(2)}, u32[]{:S(2)}) collective-permute-start(bf16[256,192]{0,1:T(8,128)(2,1)} %bitcast.79), channel_id=1, source_target_pairs={{0,8},{8,16},{16,24},{24,0},{1,9},{9,17},{17,25},{25,1},{2,10},{10... | collective-permute-start | bytes 294920 | tf_op jit(solution)/shard_map/ppermute | solution.py:418
  293.6 32.7 %collective-permute-start.44 = (bf16[256,192]{0,1:T(8,128)(2,1)}, bf16[256,192]{0,1:T(8,128)(2,1)}, u32[]{:S(2)}, u32[]{:S(2)}) collective-permute-start(bf16[256,192]{0,1:T(8,128)(2,1)} %bitcast.81), channel_id=1, source_target_pairs={{0,24},{8,0},{16,8},{24,16},{1,25},{9,1},{17,9},{25,17},{2,26},{10... | collective-permute-start | bytes 294920 | tf_op jit(solution)/shard_map/ppermute | solution.py:418
  301.6 27.3 %collective-permute-start.33 = (bf16[256,192]{0,1:T(8,128)(2,1)}, bf16[256,192]{0,1:T(8,128)(2,1)}, u32[]{:S(2)}, u32[]{:S(2)}) collective-permute-start(bf16[256,192]{0,1:T(8,128)(2,1)} %bitcast.54), channel_id=1, source_target_pairs={{0,16},{8,24},{16,0},{24,8},{1,17},{9,25},{17,1},{25,9},{2,18},{10... | collective-permute-start | bytes 294920 | tf_op jit(solution)/shard_map/ppermute | solution.py:418
  399.3 23.5 %collective-permute-start.90 = (bf16[256,192]{0,1:T(8,128)(2,1)}, bf16[256,192]{0,1:T(8,128)(2,1)}, u32[]{:S(2)}, u32[]{:S(2)}) collective-permute-start(bf16[256,192]{0,1:T(8,128)(2,1)} %bitcast.122), channel_id=1, source_target_pairs={{0,16},{8,24},{16,0},{24,8},{1,17},{9,25},{17,1},{25,9},{2,18},{10... | collective-permute-start | bytes 294920 | tf_op jit(solution)/shard_map/ppermute | solution.py:418
  401.2 25.8 %collective-permute-start.91 = (bf16[256,192]{0,1:T(8,128)(2,1)}, bf16[256,192]{0,1:T(8,128)(2,1)S(1)}, u32[]{:S(2)}, u32[]{:S(2)}) collective-permute-start(bf16[256,192]{0,1:T(8,128)(2,1)} %bitcast.124), channel_id=1, source_target_pairs={{0,8},{8,16},{16,24},{24,0},{1,9},{9,17},{17,25},{25,1},{2,10},{10... | collective-permute-start | bytes 294920 | tf_op jit(solution)/shard_map/ppermute | solution.py:418
  403.8 24.4 %collective-permute-start.92 = (bf16[256,192]{0,1:T(8,128)(2,1)}, bf16[256,192]{0,1:T(8,128)(2,1)S(1)}, u32[]{:S(2)}, u32[]{:S(2)}) collective-permute-start(bf16[256,192]{0,1:T(8,128)(2,1)} %bitcast.126), channel_id=1, source_target_pairs={{0,24},{8,0},{16,8},{24,16},{1,25},{9,1},{17,9},{25,17},{2,26},{10... | collective-permute-start | bytes 294920 | tf_op jit(solution)/shard_map/ppermute | solution.py:418
  406.7 32.9 %collective-permute-start.81 = (bf16[256,192]{0,1:T(8,128)(2,1)}, bf16[256,192]{0,1:T(8,128)(2,1)S(1)}, u32[]{:S(2)}, u32[]{:S(2)}) collective-permute-start(bf16[256,192]{0,1:T(8,128)(2,1)} %bitcast.106), channel_id=1, source_target_pairs={{0,16},{8,24},{16,0},{24,8},{1,17},{9,25},{17,1},{25,9},{2,18},{10... | collective-permute-start | bytes 294920 | tf_op jit(solution)/shard_map/ppermute | solution.py:418
  407.6 36.0 %collective-permute-start.82 = (bf16[256,192]{0,1:T(8,128)(2,1)}, bf16[256,192]{0,1:T(8,128)(2,1)S(1)}, u32[]{:S(2)}, u32[]{:S(2)}) collective-permute-start(bf16[256,192]{0,1:T(8,128)(2,1)} %bitcast.108), channel_id=1, source_target_pairs={{0,8},{8,16},{16,24},{24,0},{1,9},{9,17},{17,25},{25,1},{2,10},{10... | collective-permute-start | bytes 294920 | tf_op jit(solution)/shard_map/ppermute | solution.py:418
  427.0 29.4 %collective-permute-start.72 = (bf16[256,192]{0,1:T(8,128)(2,1)}, bf16[256,192]{0,1:T(8,128)(2,1)}, u32[]{:S(2)}, u32[]{:S(2)}) collective-permute-start(bf16[256,192]{0,1:T(8,128)(2,1)} %bitcast.90), channel_id=1, source_target_pairs={{0,16},{8,24},{16,0},{24,8},{1,17},{9,25},{17,1},{25,9},{2,18},{10... | collective-permute-start | bytes 294920 | tf_op jit(solution)/shard_map/ppermute | solution.py:418
  428.2 29.2 %collective-permute-start.73 = (bf16[256,192]{0,1:T(8,128)(2,1)}, bf16[256,192]{0,1:T(8,128)(2,1)}, u32[]{:S(2)}, u32[]{:S(2)}) collective-permute-start(bf16[256,192]{0,1:T(8,128)(2,1)} %bitcast.92), channel_id=1, source_target_pairs={{0,8},{8,16},{16,24},{24,0},{1,9},{9,17},{17,25},{25,1},{2,10},{10... | collective-permute-start | bytes 294920 | tf_op jit(solution)/shard_map/ppermute | solution.py:418
  443.6 74.7 %collective-permute-start.115 = (bf16[2,2,96,768]{3,2,1,0:T(8,128)(2,1)}, bf16[2,2,96,768]{3,2,1,0:T(8,128)(2,1)}, u32[]{:S(2)}, u32[]{:S(2)}) collective-permute-start(bf16[2,2,96,768]{3,2,1,0:T(8,128)(2,1)} %dynamic-slice_bitcast_fusion.6), channel_id=1, source_target_pairs={{0,1},{1,0},{2,3},{3,2},{4,5},{5,4},{6,7},{7,6},{8,9},{9,8},{10,11... | collective-permute-start | bytes 1769480 | tf_op jit(solution)/shard_map/ppermute | solution.py:414
  443.7 251.2 %collective-permute-start.123 = (bf16[2,2,96,3072]{3,2,1,0:T(8,128)(2,1)}, bf16[2,2,96,3072]{3,2,1,0:T(8,128)(2,1)}, u32[]{:S(2)}, u32[]{:S(2)}) collective-permute-start(bf16[2,2,96,3072]{3,2,1,0:T(8,128)(2,1)} %dynamic-slice_bitcast_fusion.1), channel_id=1, source_target_pairs={{0,1},{1,0},{2,3},{3,2},{4,5},{5,4},{6,7},{7,6},{8,9},{9,8},{10,11... | collective-permute-start | bytes 7077896 | tf_op jit(solution)/shard_map/ppermute | solution.py:414
  486.1 90.1 %collective-permute-start.96 = (bf16[256,768]{1,0:T(8,128)(2,1)}, bf16[256,768]{1,0:T(8,128)(2,1)}, u32[]{:S(2)}, u32[]{:S(2)}) collective-permute-start(bf16[256,768]{1,0:T(8,128)(2,1)} %get-tuple-element.102), channel_id=1, source_target_pairs={{24,16},{25,17},{26,18},{27,19},{28,20},{29,21},{30,22},{31,23}} | collective-permute-start | bytes 1179656 | tf_op jit(solution)/shard_map/ppermute | solution.py:512
  552.6 29.1 %collective-permute-start.87 = (bf16[256,768]{1,0:T(8,128)(2,1)}, bf16[256,768]{1,0:T(8,128)(2,1)}, u32[]{:S(2)}, u32[]{:S(2)}) collective-permute-start(bf16[256,768]{1,0:T(8,128)(2,1)} %get-tuple-element.98), channel_id=1, source_target_pairs={{24,16},{25,17},{26,18},{27,19},{28,20},{29,21},{30,22},{31,23}} | collective-permute-start | bytes 1179656 | tf_op jit(solution)/shard_map/ppermute | solution.py:512
  555.1 22.0 %collective-permute-start.94 = (bf16[256,768]{1,0:T(8,128)(2,1)}, bf16[256,768]{1,0:T(8,128)(2,1)}, u32[]{:S(2)}, u32[]{:S(2)}) collective-permute-start(bf16[256,768]{1,0:T(8,128)(2,1)} %fusion.42), channel_id=1, source_target_pairs={{0,8},{8,16},{1,9},{9,17},{2,10},{10,18},{3,11},{11,19},{4,12},{12... | collective-permute-start | bytes 1179656 | tf_op jit(solution)/shard_map/ppermute | solution.py:511
  577.1 23.4 %collective-permute-start.76 = (bf16[256,768]{1,0:T(8,128)(2,1)}, bf16[256,768]{1,0:T(8,128)(2,1)S(1)}, u32[]{:S(2)}, u32[]{:S(2)}) collective-permute-start(bf16[256,768]{1,0:T(8,128)(2,1)} %fusion.52), channel_id=1, source_target_pairs={{0,8},{8,16},{1,9},{9,17},{2,10},{10,18},{3,11},{11,19},{4,12},{12... | collective-permute-start | bytes 1179656 | tf_op jit(solution)/shard_map/ppermute | solution.py:511
  584.1 25.3 %collective-permute-start.97 = (bf16[256,768]{1,0:T(8,128)(2,1)S(1)}, bf16[256,768]{1,0:T(8,128)(2,1)S(1)}, u32[]{:S(2)}, u32[]{:S(2)}) collective-permute-start(bf16[256,768]{1,0:T(8,128)(2,1)S(1)} %get-tuple-element.100), channel_id=1, source_target_pairs={{16,8},{24,16},{17,9},{25,17},{18,10},{26,18},{19,11},{27,19},{20,... | collective-permute-start | bytes 1179656 | tf_op jit(solution)/shard_map/ppermute | solution.py:512
  605.1 34.1 %collective-permute-start.86 = (bf16[256,768]{1,0:T(8,128)(2,1)S(1)}, bf16[256,768]{1,0:T(8,128)(2,1)S(1)}, u32[]{:S(2)}, u32[]{:S(2)}) collective-permute-start(bf16[256,768]{1,0:T(8,128)(2,1)S(1)} %get-tuple-element.95), channel_id=1, source_target_pairs={{0,8},{8,16},{16,24},{1,9},{9,17},{17,25},{2,10},{10,18},{18,26},{... | collective-permute-start | bytes 1179656 | tf_op jit(solution)/shard_map/ppermute | solution.py:511
  610.2 27.3 %collective-permute-start.98 = (bf16[256,768]{1,0:T(8,128)(2,1)S(1)}, bf16[256,768]{1,0:T(8,128)(2,1)S(1)}, u32[]{:S(2)}, u32[]{:S(2)}) collective-permute-start(bf16[256,768]{1,0:T(8,128)(2,1)S(1)} %fusion.41), channel_id=1, source_target_pairs={{8,0},{16,8},{24,16},{9,1},{17,9},{25,17},{10,2},{18,10},{26,18},{... | collective-permute-start | bytes 1179656 | tf_op jit(solution)/shard_map/ppermute | solution.py:512
  611.6 29.9 %collective-permute-start.89 = (bf16[256,768]{1,0:T(8,128)(2,1)S(1)}, bf16[256,768]{1,0:T(8,128)(2,1)S(1)}, u32[]{:S(2)}, u32[]{:S(2)}) collective-permute-start(bf16[256,768]{1,0:T(8,128)(2,1)S(1)} %fusion.46), channel_id=1, source_target_pairs={{8,0},{16,8},{24,16},{9,1},{17,9},{25,17},{10,2},{18,10},{26,18},{... | collective-permute-start | bytes 1179656 | tf_op jit(solution)/shard_map/ppermute | solution.py:512
  613.0 29.8 %collective-permute-start.77 = (bf16[256,768]{1,0:T(8,128)(2,1)S(1)}, bf16[256,768]{1,0:T(8,128)(2,1)S(1)}, u32[]{:S(2)}, u32[]{:S(2)}) collective-permute-start(bf16[256,768]{1,0:T(8,128)(2,1)S(1)} %get-tuple-element.88), channel_id=1, source_target_pairs={{0,8},{8,16},{16,24},{1,9},{9,17},{17,25},{2,10},{10,18},{18,26},{... | collective-permute-start | bytes 1179656 | tf_op jit(solution)/shard_map/ppermute | solution.py:511
  639.2 61.4 %collective-permute-start.131 = (bf16[2,2,384,768]{3,2,1,0:T(8,128)(2,1)}, bf16[2,2,384,768]{3,2,1,0:T(8,128)(2,1)}, u32[]{:S(2)}, u32[]{:S(2)}) collective-permute-start(bf16[2,2,384,768]{3,2,1,0:T(8,128)(2,1)} %dynamic-slice_bitcast_fusion), channel_id=1, source_target_pairs={{0,1},{1,0},{2,3},{3,2},{4,5},{5,4},{6,7},{7,6},{8,9},{9,8},{10,11... | collective-permute-start | bytes 7077896 | tf_op jit(solution)/shard_map/ppermute | solution.py:414
  693.6 50.0 %collective-permute-start.106 = (bf16[8,96]{1,0:T(8,128)(2,1)S(1)}, bf16[8,96]{1,0:T(8,128)(2,1)S(1)}, u32[]{:S(2)}, u32[]{:S(2)}) collective-permute-start(bf16[8,96]{1,0:T(8,128)(2,1)S(1)} %add_convert_fusion.6), channel_id=1, source_target_pairs={{0,8},{8,0},{16,24},{24,16},{1,9},{9,1},{17,25},{25,17},{2,10},{10... | collective-permute-start | bytes 4616 | tf_op jit(solution)/shard_map/ppermute | solution.py:414
  704.6 22.0 %collective-permute-start.132 = (bf16[2,192,768]{2,1,0:T(8,128)(2,1)S(1)}, bf16[2,192,768]{2,1,0:T(8,128)(2,1)S(1)}, u32[]{:S(2)}, u32[]{:S(2)}) collective-permute-start(bf16[2,192,768]{2,1,0:T(8,128)(2,1)S(1)} %dynamic-slice_bitcast_fusion.3), channel_id=1, source_target_pairs={{0,2},{1,3},{2,0},{3,1},{4,6},{5,7},{6,4},{7,5},{8,10},{9,11},{10,... | collective-permute-start | bytes 1769480 | tf_op jit(solution)/shard_map/ppermute | solution.py:414
  (172 other events, 1822.7 us)
